TPU v7x, 32 devices: a whole 2x2x4 slice. The times are simulated.
32 devices in a mesh: mp: 2 (over x), tok: 2 (over core), lat: 8 (over z, y).
Axes of the slice: x: 2, y: 2, z: 4, core: 2. Of those that a mesh axis runs over, the one named last changes fastest.
Arguments:
- inputs: bfloat16 [2, 384, 4608], P('mp', 'lat', 'tok'), may hold values from -6 to 6
- gate_w: bfloat16 [2, 4608, 18432], P('mp', 'tok', 'lat'), may hold values from -0.09375 to 0.09375
- up_w: bfloat16 [2, 4608, 18432], P('mp', 'tok', 'lat'), may hold values from -0.09375 to 0.09375
- down_w: bfloat16 [2, 18432, 4608], P('mp', 'lat', 'tok'), may hold values from -0.046875 to 0.046875
- enc_w: bfloat16 [2, 4608, 8192], P('mp', 'tok', 'lat'), may hold values from -0.0625 to 0.0625
- enc_bias: float32 [8192], P('lat'), may hold values from -3 to 3
- dec_w: bfloat16 [8192, 2, 4608], P('lat', 'mp', 'tok'), may hold values from -0.0625 to 0.0625
- dec_bias: float32 [2, 4608], P('mp', 'tok'), may hold values from -3 to 3
Outputs:
- recon_error: float32 [2, 384, 4608], P('mp', 'lat', 'tok')
- dec_grad: float32 [8192, 2, 4608], P('lat', 'mp', 'tok')
- latent_grad: float32 [384, 8192], P(None, 'lat')
All inputs are finite; a program needn't handle non-finite values.
Results may differ from a plain program's by a relative error of at most 0.009.
Values may be sent and summed in bfloat16 or wider, within the bound.
No kernel may reach another device: no remote copies, remote signals or barrier semaphores. Data moves between devices by JAX's collectives and lax.ppermute only.
A program may use at most 128 MiB of HBM per device.

v0:
```python
import jax
import jax.numpy as jnp
from jax import lax
from jax.sharding import PartitionSpec as P


def contract_rows(left, right):
    return lax.dot_general(
        left, right, (((0,), (0,)), ((), ())), preferred_element_type=jnp.float32
    )


def contract_cols(left, right):
    return lax.dot_general(
        left, right, (((1,), (1,)), ((), ())), preferred_element_type=jnp.float32
    )


def body(inputs, gate_w, up_w, down_w, enc_w, enc_bias, dec_w, dec_bias):
    x_rows = inputs[0]
    gathered = lax.all_gather(x_rows, "lat", axis=0, tiled=True)
    gate_local = gate_w[0]
    up_local = up_w[0]
    width = gate_local.shape[1]
    block = gathered
    both = lax.psum_scatter(
        jnp.concatenate(
            [
                jnp.dot(block, gate_local, preferred_element_type=jnp.float32),
                jnp.dot(block, up_local, preferred_element_type=jnp.float32),
            ],
            axis=1,
        ),
        "tok",
        scatter_dimension=0,
        tiled=True,
    )
    hidden = (jax.nn.gelu(both[:, :width], approximate=True) * both[:, width:]).astype(jnp.bfloat16)
    hidden_all = lax.all_gather(hidden, "tok", axis=0, tiled=True)
    down_local = down_w[0]
    block = hidden_all
    acts = lax.psum_scatter(
        jnp.dot(block, down_local, preferred_element_type=jnp.float32),
        "lat",
        scatter_dimension=0,
        tiled=True,
    ).astype(jnp.bfloat16)
    acts_all = lax.all_gather(acts, "lat", axis=0, tiled=True)
    partial_pre = jnp.dot(acts_all, enc_w[0], preferred_element_type=jnp.float32)
    pre = lax.psum(partial_pre, ("mp", "tok"))
    codes = jnp.maximum(pre + enc_bias, 0.0).astype(jnp.bfloat16)
    decoder = dec_w[:, 0, :]
    bias_row = dec_bias[0]
    block = codes
    recon = lax.psum_scatter(
        jnp.dot(block, decoder, preferred_element_type=jnp.float32),
        "lat",
        scatter_dimension=0,
        tiled=True,
    )
    error = recon + bias_row - acts.astype(jnp.float32)
    error_all = lax.all_gather(error.astype(jnp.bfloat16), "lat", axis=0, tiled=True)
    decoder_grad = contract_rows(codes, error_all)
    latent_grad = lax.psum(contract_cols(error_all, decoder), ("mp", "tok"))
    return (error[None], decoder_grad[:, None, :], latent_grad)


def solution(mesh):
    in_specs = (
        P("mp", "lat", "tok"),
        P("mp", "tok", "lat"),
        P("mp", "tok", "lat"),
        P("mp", "lat", "tok"),
        P("mp", "tok", "lat"),
        P("lat"),
        P("lat", "mp", "tok"),
        P("mp", "tok"),
    )
    out_specs = (P("mp", "lat", "tok"), P("lat", "mp", "tok"), P(None, "lat"))
    return jax.shard_map(body, mesh=mesh, in_specs=in_specs, out_specs=out_specs, check_vma=False)
```

profile of v0, /device:TPU:0, one launch (start us, length us, event | category | flops | bytes accessed | tf_op | source)
XLA Modules:
  0.0 503.1 jit_solution(12187527069317198368)
XLA Ops:
  7.2 0.7 all-gather.12.cloned.1.call-update
  7.9 50.9 %all-gather.12.cloned.1.call-done = bf16[1,384,2304]{2,1,0:T(8,128)(2,1)} async-done(((bf16[1,48,2304]{2,1,0:T(8,128)(2,1)}), bf16[1,384,2304]{2,1,0:T(8,128)(2,1)}) %all-gather.12.cloned.1.call-update) | async-done | bytes 1769488 | tf_op jit(solution)/shard_map/all_gather | solution.py:21
  58.8 9.3 %fusion.2 = f32[384,2304]{1,0:T(8,128)S(1)} fusion(bf16[1,2304,2304]{2,1,0:T(8,128)(2,1)} %param.10, bf16[1,384,2304]{2,1,0:T(8,128)(2,1)} %all-gather.12.cloned.1.call-done), kind=kOutput, calls=%fused_computation.2 | convolution fusion | flops 4076863488 | bytes 15925248 | tf_op jit(solution)/shard_map/dot_general | solution.py:30
  68.2 7.4 %fusion.4 = f32[384,2304]{1,0:T(8,128)S(1)} fusion(bf16[1,2304,2304]{2,1,0:T(8,128)(2,1)} %param.9, bf16[1,384,2304]{2,1,0:T(8,128)(2,1)S(1)} %copy-done.5), kind=kOutput, calls=%fused_computation.4 | convolution fusion | flops 4076863488 | bytes 15925248 | tf_op jit(solution)/shard_map/dot_general | solution.py:29
  75.7 4.0 pad_maximum_fusion
  79.7 14.5 %reduce-scatter.4.cloned.1.call-done = f32[192,4608]{1,0:T(8,128)} async-done(((f32[384,4608]{1,0:T(8,128)}), f32[192,4608]{1,0:T(8,128)}) %reduce-scatter.4.cloned.1.call-update) | async-done | bytes 3538960 | tf_op jit(solution)/shard_map/reduce_scatter | solution.py:26
  94.2 3.5 fusion.20
  97.8 11.5 %all-gather.6.cloned.1.call-done = bf16[384,2304]{1,0:T(8,128)(2,1)} async-done(((bf16[192,2304]{1,0:T(8,128)(2,1)}), bf16[384,2304]{1,0:T(8,128)(2,1)}) %all-gather.6.cloned.1.call-update) | async-done | bytes 1769488 | tf_op jit(solution)/shard_map/all_gather | solution.py:39
  109.3 10.6 %fusion = f32[384,2304]{1,0:T(8,128)} fusion(bf16[384,2304]{1,0:T(8,128)(2,1)} %all-gather.6.cloned.1.call-done, bf16[1,2304,2304]{2,1,0:T(8,128)(2,1)} %param.11), kind=kOutput, calls=%fused_computation | convolution fusion | flops 4076863488 | bytes 15925248 | tf_op jit(solution)/shard_map/dot_general | solution.py:43
  120.0 80.4 %reduce-scatter.6.cloned.1.call-done = f32[48,2304]{1,0:T(8,128)} async-done(((f32[384,2304]{1,0:T(8,128)}), f32[48,2304]{1,0:T(8,128)}) %reduce-scatter.6.cloned.1.call-update) | async-done | bytes 442384 | tf_op jit(solution)/shard_map/reduce_scatter | solution.py:42
  200.5 1.7 convert_element_type.16
  202.3 46.6 %all-gather.8.cloned.1.call-done = bf16[384,2304]{1,0:T(8,128)(2,1)} async-done(((bf16[48,2304]{1,0:T(8,128)(2,1)}), bf16[384,2304]{1,0:T(8,128)(2,1)}) %all-gather.8.cloned.1.call-update) | async-done | bytes 1769488 | tf_op jit(solution)/shard_map/all_gather | solution.py:48
  248.8 6.0 %fusion.10 = f32[384,1024]{1,0:T(8,128)} fusion(bf16[384,2304]{1,0:T(8,128)(2,1)} %all-gather.8.cloned.1.call-done, bf16[1,2304,1024]{2,1,0:T(8,128)(2,1)} %param.12), kind=kOutput, calls=%fused_computation.12 | convolution fusion | flops 1811939328 | bytes 8060928 | tf_op jit(solution)/shard_map/dot_general | solution.py:49
  254.9 42.0 %all-reduce.3.cloned.1.call-done = f32[384,1024]{1,0:T(8,128)} async-done(((f32[384,1024]{1,0:T(8,128)}), f32[384,1024]{1,0:T(8,128)}) %all-reduce.3.cloned.1.call-update) | async-done | bytes 1572880 | tf_op jit(solution)/shard_map/psum | solution.py:50
  296.9 6.6 %fusion.8 = f32[384,2304]{1,0:T(8,128)} fusion(bf16[1024,1,2304]{2,0,1:T(8,128)(2,1)} %param.14, f32[384,1024]{1,0:T(8,128)} %all-reduce.3.cloned.1.call-done, f32[1024]{0:T(1024)S(1)} %copy-done.3), kind=kOutput, calls=%fused_computation.10 | convolution fusion | flops 1813118976 | bytes 9834496 | tf_op jit(solution)/shard_map/dot_general | solution.py:56
  303.6 0.6 copy-done.4
  304.2 78.7 %reduce-scatter.8.cloned.1.call-done = f32[48,2304]{1,0:T(8,128)} async-done(((f32[384,2304]{1,0:T(8,128)}), f32[48,2304]{1,0:T(8,128)}) %reduce-scatter.8.cloned.1.call-update) | async-done | bytes 442384 | tf_op jit(solution)/shard_map/reduce_scatter | solution.py:55
  382.9 1.9 fusion.23
  385.0 46.4 %all-gather.10.cloned.1.call-done = bf16[384,2304]{1,0:T(8,128)(2,1)} async-done(((bf16[48,2304]{1,0:T(8,128)(2,1)}), bf16[384,2304]{1,0:T(8,128)(2,1)}) %all-gather.10.cloned.1.call-update) | async-done | bytes 1769488 | tf_op jit(solution)/shard_map/all_gather | solution.py:62
  431.4 6.2 %fusion.6 = f32[384,1024]{1,0:T(8,128)} fusion(bf16[384,2304]{1,0:T(8,128)(2,1)} %all-gather.10.cloned.1.call-done, bf16[1024,1,2304]{2,0,1:T(8,128)(2,1)} %param.14), kind=kOutput, calls=%fused_computation.8 | convolution fusion | flops 1811939328 | bytes 8060928 | tf_op jit(solution)/shard_map/dot_general | solution.py:14
  437.6 1.4 copy-done.2
  439.0 2.7 convolution_bitcast_fusion
  441.6 52.2 %copy.11 = f32[1024,1,2304]{2,1,0:T(1,128)} copy(f32[1024,1,2304]{2,0,1:T(8,128)S(1)} %convolution_bitcast_fusion) | data formatting | bytes 18874368
  493.9 2.7 copy.14
  (29 shorter events, 0.7 us)
Async XLA Ops:
  7.2 51.7 %all-gather.12.cloned.1.call-start = ((), (), s32[]{:S(2)}) async-start(), calls=%async_computation.11 | async-start | bytes 1990656 | tf_op jit(solution)/shard_map/all_gather | solution.py:21
  7.9 86.3 %reduce-scatter.4.cloned.1.call-start = ((), (), s32[]{:S(2)}) async-start(), calls=%async_computation.3 | async-start | bytes 10616832 | tf_op jit(solution)/shard_map/reduce_scatter | solution.py:26
  58.8 9.3 %copy-start.5 = (bf16[1,384,2304]{2,1,0:T(8,128)(2,1)S(1)}, bf16[1,384,2304]{2,1,0:T(8,128)(2,1)}, u32[]{:S(2)}) copy-start(bf16[1,384,2304]{2,1,0:T(8,128)(2,1)} %all-gather.12.cloned.1.call-done) | copy-start | bytes 5308420
  79.6 29.7 %all-gather.6.cloned.1.call-start = ((), (), s32[]{:S(2)}) async-start(), calls=%async_computation.4 | async-start | bytes 2654208 | tf_op jit(solution)/shard_map/all_gather | solution.py:39
  97.8 102.7 %reduce-scatter.6.cloned.1.call-start = ((), (), s32[]{:S(2)}) async-start(), calls=%async_computation.5 | async-start | bytes 3981312 | tf_op jit(solution)/shard_map/reduce_scatter | solution.py:42
  120.0 128.9 %all-gather.8.cloned.1.call-start = ((), (), s32[]{:S(2)}) async-start(), calls=%async_computation.6 | async-start | bytes 1990656 | tf_op jit(solution)/shard_map/all_gather | solution.py:48
  202.2 94.7 %copy-start.3 = (f32[1024]{0:T(1024)S(1)}, f32[1024]{0:T(1024)}, u32[]{:S(2)}) copy-start(f32[1024]{0:T(1024)} %param.13) | copy-start | bytes 12292
  202.2 94.7 %all-reduce.3.cloned.1.call-start = ((), (), s32[]{:S(2)}) async-start(), calls=%async_computation.7 | async-start | bytes 3145728 | tf_op jit(solution)/shard_map/psum | solution.py:50
  254.9 128.0 %reduce-scatter.8.cloned.1.call-start = ((), (), s32[]{:S(2)}) async-start(), calls=%async_computation.8 | async-start | bytes 3981312 | tf_op jit(solution)/shard_map/reduce_scatter | solution.py:55
  303.5 0.7 copy-start.4
  303.5 79.4 %copy-start.1 = (f32[48,2304]{1,0:T(8,128)S(1)}, f32[48,2304]{1,0:T(8,128)}, u32[]{:S(2)}) copy-start(f32[48,2304]{1,0:T(8,128)} %reduce-scatter.6.cloned.1.call-done) | copy-start | bytes 1327108
  303.5 127.9 %all-gather.10.cloned.1.call-start = ((), (), s32[]{:S(2)}) async-start(), calls=%async_computation.9 | async-start | bytes 1990656 | tf_op jit(solution)/shard_map/all_gather | solution.py:62
  384.8 109.1 %all-reduce.5.cloned.1.call-start = ((), (), s32[]{:S(2)}) async-start(), calls=%async_computation.10 | async-start | bytes 3145728 | tf_op jit(solution)/shard_map/psum | solution.py:64
  431.4 6.2 %copy-start = (bf16[384,2304]{1,0:T(8,128)(2,1)S(1)}, bf16[384,2304]{1,0:T(8,128)(2,1)}, u32[]{:S(2)}) copy-start(bf16[384,2304]{1,0:T(8,128)(2,1)} %all-gather.10.cloned.1.call-done) | copy-start | bytes 5308420
  437.6 1.4 copy-start.2
Sparse Core Ops, SparseCore 0:
  10.2 48.6 all-gather.11
  79.8 14.4 reduce-scatter.3
  97.9 11.3 all-gather.5
  120.1 80.3 reduce-scatter.5
  203.3 45.4 all-gather.7
  255.0 41.8 all-reduce.2
  303.7 79.1 reduce-scatter.7
  385.9 45.4 all-gather.9
  437.7 41.8 all-reduce.4
where the time goes:
time: 503 us
  waiting for transfers between devices  372 us (74%)
  local copies, waits for them, and re-layouts  57 us (11%)
  matrix products  48.9 us (10%)
  between operations  13.9 us (3%)
  other arithmetic  11.1 us (2%)
    reduce_scatter x1, waiting for transfers between devices, body(): lax.psum_scatter(jnp.dot(block, down_local, preferred_element_type=jnp.fl...  80.4 us
    reduce_scatter x1, waiting for transfers between devices, body(): lax.psum_scatter(jnp.dot(block, decoder, preferred_element_type=jnp.float...  78.7 us
    unnamed x14, local copies, waits for them, and re-layouts  57 us
    all_gather x1, waiting for transfers between devices, body(): gathered = lax.all_gather(x_rows, 'lat', axis=0, tiled=True)  50.9 us
    all_gather x1, waiting for transfers between devices, body(): acts_all = lax.all_gather(acts, 'lat', axis=0, tiled=True)  46.6 us
    all_gather x1, waiting for transfers between devices, body(): lax.all_gather(error.astype(jnp.bfloat16), 'lat', axis=0, tiled=True)  46.4 us
    psum x1, waiting for transfers between devices, body(): pre = lax.psum(partial_pre, ('mp', 'tok'))  42 us
    reduce_scatter x1, waiting for transfers between devices, body(): lax.psum_scatter(jnp.concatenate([jnp.dot(block, gate_local, preferred_el...  14.5 us
  transfers between devices with their start and end apart: 9, of which 8 were waited for; matrix products, arithmetic and copies ran while one was open for 11% of the time, Pallas kernels for 0%

commit v1 on v0

--- a/solution.py
+++ b/solution.py
@@ -1,22 +1,129 @@
 import jax
 import jax.numpy as jnp
 from jax import lax
+from jax.experimental import pallas as pl
+from jax.experimental.pallas import tpu as pltpu
 from jax.sharding import PartitionSpec as P
+
+F32, BF16 = jnp.float32, jnp.bfloat16
+HALVES = ((0, 3), (1, 2))
+SWAP2 = [(0, 1), (1, 0)]
+
+
+def dot(a, b):
+    return jnp.dot(a, b, preferred_element_type=F32)
 
 
 def contract_rows(left, right):
-    return lax.dot_general(
-        left, right, (((0,), (0,)), ((), ())), preferred_element_type=jnp.float32
-    )
+    return lax.dot_general(left, right, (((0,), (0,)), ((), ())), preferred_element_type=F32)
 
 
 def contract_cols(left, right):
-    return lax.dot_general(
-        left, right, (((1,), (1,)), ((), ())), preferred_element_type=jnp.float32
-    )
+    return lax.dot_general(left, right, (((1,), (1,)), ((), ())), preferred_element_type=F32)
+
+
+def swap(x, k):
+    return lax.ppermute(x, "lat", [(i, i ^ k) for i in range(8)])
+
+
+def gather(x):
+    got = {0: x}
+    for z in (3, 1, 2):
+        got[z] = swap(x, 2 * z)
+    other = {z: swap(got[z], 1) for z in (0, 1, 3, 2)}
+    return [jnp.concatenate([b for z in half for b in (got[z], other[z])], axis=0) for half in HALVES]
+
+
+def scatter_half(p, half, rows):
+    terms = []
+    for j in (1, 0):
+        z = half[j]
+        mine = p[2 * j * rows:(2 * j + 1) * rows]
+        away = p[(2 * j + 1) * rows:(2 * j + 2) * rows].astype(BF16)
+        s = mine + swap(away, 1).astype(F32)
+        terms.append(s if z == 0 else swap(s.astype(BF16), 2 * z).astype(F32))
+    return terms
+
+
+def pair_sum(p, axis):
+    b = p.astype(BF16)
+    return b.astype(F32) + lax.ppermute(b, axis, SWAP2).astype(F32)
+
+
+def half_sum(p, tok):
+    h = p.shape[0] // 2
+    lo, hi = p[:h], p[h:]
+    mine = jnp.where(tok == 0, lo, hi)
+    other = jnp.where(tok == 0, hi, lo)
+    return mine + lax.ppermute(other.astype(BF16), "tok", SWAP2).astype(F32)
+
+
+def join(h, tok):
+    o = lax.ppermute(h, "tok", SWAP2)
+    return jnp.concatenate([jnp.where(tok == 0, h, o), jnp.where(tok == 0, o, h)], axis=0)
+
+
+def grad_kernel(c0, c1, e0, e1, out):
+    n, w = c0.shape[1], e0.shape[1]
+    cols = w // 128
+    r = contract_rows(c0[...], e0[...]) + contract_rows(c1[...], e1[...])
+    for c in range(cols):
+        out[pl.ds(c, n, cols), :] = r[:, c * 128:(c + 1) * 128]
+
+
+def decoder_grad(codes, errs):
+    rows, n = codes[0].shape
+    w = errs[0].shape[1]
+    step = 128
+    cspec = pl.BlockSpec((rows, step), lambda i: (0, i))
+    espec = pl.BlockSpec((rows, w), lambda i: (0, 0))
+    out = pl.pallas_call(
+        grad_kernel,
+        grid=(n // step,),
+        in_specs=[cspec, cspec, espec, espec],
+        out_specs=pl.BlockSpec((step * w // 128, 128), lambda i: (i, 0)),
+        out_shape=jax.ShapeDtypeStruct((n * w // 128, 128), F32),
+        compiler_params=pltpu.CompilerParams(vmem_limit_bytes=24 << 20),
+        cost_estimate=pl.CostEstimate(flops=4 * rows * n * w, bytes_accessed=4 * n * w, transcendentals=0),
+    )(*codes, *errs)
+    return out.reshape(n, 1, w)
 
 
 def body(inputs, gate_w, up_w, down_w, enc_w, enc_bias, dec_w, dec_bias):
+    me = lax.axis_index("lat")
+    tok = lax.axis_index("tok")
+    gate_l, up_l, down_l, enc_l = gate_w[0], up_w[0], down_w[0], enc_w[0]
+    dec_l = dec_w[:, 0, :]
+    rows = inputs.shape[1]
+    terms = []
+    for xa, half in zip(gather(inputs[0]), HALVES):
+        g = half_sum(dot(xa, gate_l), tok)
+        u = half_sum(dot(xa, up_l), tok)
+        hid = join((jax.nn.gelu(g, approximate=True) * u).astype(BF16), tok)
+        terms += scatter_half(dot(hid, down_l), half, rows)
+    acts = sum(terms).astype(BF16)
+    codes, terms = [], []
+    for aa, half in zip(gather(acts), HALVES):
+        pre = pair_sum(pair_sum(dot(aa, enc_l), "tok"), "mp")
+        codes.append(jnp.maximum(pre + enc_bias, 0.0).astype(BF16))
+        terms += scatter_half(dot(codes[-1], dec_l), half, rows)
+    err = sum(terms) + dec_bias[0] - acts.astype(F32)
+    errs = gather(err.astype(BF16))
+    lat = {}
+    for e, half in zip(errs, HALVES):
+        l = pair_sum(pair_sum(contract_cols(e, dec_l), "tok"), "mp").reshape(2, 2, rows, -1)
+        for j, z in enumerate(half):
+            lat[z] = l[j]
+    dec_grad = decoder_grad(codes, errs)
+    la = jnp.stack([lat[z] for z in range(4)], axis=0).reshape(8, rows, -1)
+    for bit in (1, 2, 4):
+        sw = la.reshape(8 // (2 * bit), 2, bit, *la.shape[1:])[:, ::-1].reshape(la.shape)
+        la = jnp.where((me & bit) != 0, sw, la)
+    latent = la.reshape(8 * rows, -1)
+    return (err[None], dec_grad, latent)
+
+
+def plain_body(inputs, gate_w, up_w, down_w, enc_w, enc_bias, dec_w, dec_bias):
     x_rows = inputs[0]
     gathered = lax.all_gather(x_rows, "lat", axis=0, tiled=True)
     gate_local = gate_w[0]
@@ -66,6 +173,8 @@
 
 
 def solution(mesh):
+    sizes = [mesh.shape[a] for a in ("mp", "tok", "lat")]
+    step = body if sizes == [2, 2, 8] else plain_body
     in_specs = (
         P("mp", "lat", "tok"),
         P("mp", "tok", "lat"),
@@ -77,4 +186,4 @@
         P("mp", "tok"),
     )
     out_specs = (P("mp", "lat", "tok"), P("lat", "mp", "tok"), P(None, "lat"))
-    return jax.shard_map(body, mesh=mesh, in_specs=in_specs, out_specs=out_specs, check_vma=False)
+    return jax.shard_map(step, mesh=mesh, in_specs=in_specs, out_specs=out_specs, check_vma=False)

time: 503 us -> 240 us (0.48)
  waiting for transfers between devices: 372 us -> 123 us
  starting transfers between devices: 0.55 us -> 62.5 us
  local copies, waits for them, and re-layouts: 57 us -> 6.44 us
  matrix products: 48.9 us -> 27.9 us
  between operations: 13.9 us -> 1.36 us
  Pallas kernels: 0 us -> 6.69 us
    reduce_scatter x3 -> x0, waiting for transfers between devices: 174 us -> none  [the longest x1 80.4 us: body(): lax.psum_scatter(jnp.dot(block, down_local, preferred_element_type=jnp.fl...]
    all_gather x4 -> x0, waiting for transfers between devices: 155 us -> none  [the longest x1 50.9 us: body(): gathered = lax.all_gather(x_rows, 'lat', axis=0, tiled=True)]
    ppermute x0 -> x49, waiting for transfers between devices: none -> 123 us  [the longest x35 94.5 us: swap(): return lax.ppermute(x, 'lat', [(i, i ^ k) for i in range(8)])]
    ppermute x0 -> x49, starting transfers between devices: none -> 62.5 us  [the longest x35 54.9 us: swap(): return lax.ppermute(x, 'lat', [(i, i ^ k) for i in range(8)])]
    unnamed x14 -> x44, local copies, waits for them, and re-layouts: 57 us -> 2.55 us
    psum x2 -> x0, waiting for transfers between devices: 42 us -> none  [the longest x1 42 us: body(): pre = lax.psum(partial_pre, ('mp', 'tok'))]
    dot_general x6 -> x10, matrix products: 42.7 us -> 22.2 us  [dot(): return jnp.dot(a, b, preferred_element_type=F32)]
    pallas_call x0 -> x1, Pallas kernels: none -> 6.69 us  [decoder_grad(): pl.pallas_call(grad_kernel, grid=(n // step,), in_specs=[cspec, cspec, es...]
  transfers between devices with their start and end apart: 9 -> 49, of which waited for: 8 -> 23; matrix products, arithmetic and copies ran while one was open for 11% -> 13% of each run, Pallas kernels for 0% -> 3%
where the time goes in v1:
time: 240 us
  waiting for transfers between devices  123 us (51%)
  starting transfers between devices  62.5 us (26%)
  matrix products  27.9 us (12%)
  other arithmetic  11.4 us (5%)
  Pallas kernels  6.69 us (3%)
  local copies, waits for them, and re-layouts  6.44 us (3%)
    ppermute x35, waiting for transfers between devices, swap(): return lax.ppermute(x, 'lat', [(i, i ^ k) for i in range(8)])  94.5 us
    ppermute x35, starting transfers between devices, swap(): return lax.ppermute(x, 'lat', [(i, i ^ k) for i in range(8)])  54.9 us
    ppermute x8, waiting for transfers between devices, pair_sum(): return b.astype(F32) + lax.ppermute(b, axis, SWAP2).astype(F32)  27 us
    dot_general x10, matrix products, dot(): return jnp.dot(a, b, preferred_element_type=F32)  22.2 us
    pallas_call x1, Pallas kernels, decoder_grad(): pl.pallas_call(grad_kernel, grid=(n // step,), in_specs=[cspec, cspec, es...  6.69 us
    ppermute x8, starting transfers between devices, pair_sum(): return b.astype(F32) + lax.ppermute(b, axis, SWAP2).astype(F32)  6.11 us
    dot_general x2, matrix products, contract_cols(): lax.dot_general(left, right, (((1,), (1,)), ((), ())), preferred_element_...  5.68 us
  transfers between devices with their start and end apart: 49, of which 23 were waited for; matrix products, arithmetic and copies ran while one was open for 13% of the time, Pallas kernels for 3%

profile of v1, /device:TPU:0, one launch (start us, length us, event | category | flops | bytes accessed | tf_op | source)
XLA Modules:
  0.0 239.7 jit_solution(5699313312540506437)
XLA Ops:
  0.6 4.1 %collective-permute-start.11 = (bf16[48,2304]{1,0:T(8,128)(2,1)}, bf16[48,2304]{1,0:T(8,128)(2,1)S(1)}, u32[]{:S(2)}, u32[]{:S(2)}) collective-permute-start(bf16[48,2304]{1,0:T(8,128)(2,1)} %bitcast.89), channel_id=1, source_target_pairs={{0,4},{1,5},{2,6},{3,7},{4,0},{5,1},{6,2},{7,3},{8,12},{9,13},{10,... | collective-permute-start | bytes 663560 | tf_op jit(solution)/shard_map/ppermute | solution.py:26
  8.1 8.8 %collective-permute-done.11 = bf16[48,2304]{1,0:T(8,128)(2,1)S(1)} collective-permute-done((bf16[48,2304]{1,0:T(8,128)(2,1)}, bf16[48,2304]{1,0:T(8,128)(2,1)S(1)}, u32[]{:S(2)}, u32[]{:S(2)}) %collective-permute-start.11) | collective-permute-done | bytes 221216 | tf_op jit(solution)/shard_map/ppermute | solution.py:26
  16.9 5.7 %collective-permute-start.12 = (bf16[48,2304]{1,0:T(8,128)(2,1)S(1)}, bf16[48,2304]{1,0:T(8,128)(2,1)S(1)}, u32[]{:S(2)}, u32[]{:S(2)}) collective-permute-start(bf16[48,2304]{1,0:T(8,128)(2,1)S(1)} %collective-permute-done.11), channel_id=1, source_target_pairs={{0,1},{1,0},{2,3},{3,2},{4,5},{5,4},{6,7},{7,6},{8,9},{9,8},{10,11... | collective-permute-start | bytes 663560 | tf_op jit(solution)/shard_map/ppermute | solution.py:26
  24.6 5.1 %collective-permute-done.10 = bf16[48,2304]{1,0:T(8,128)(2,1)S(1)} collective-permute-done((bf16[48,2304]{1,0:T(8,128)(2,1)S(1)}, bf16[48,2304]{1,0:T(8,128)(2,1)S(1)}, u32[]{:S(2)}, u32[]{:S(2)}) %collective-permute-start.10) | collective-permute-done | bytes 221216 | tf_op jit(solution)/shard_map/ppermute | solution.py:26
  29.8 6.4 %fusion.4 = f32[192,2304]{1,0:T(8,128)S(1)} fusion(bf16[192,2304]{1,0:T(8,128)(2,1)S(1)} %constant_dynamic-update-slice_fusion, bf16[1,2304,2304]{2,1,0:T(8,128)(2,1)} %param.10), kind=kOutput, calls=%fused_computation.4 | convolution fusion | flops 2038431744 | bytes 13271040 | tf_op jit(solution)/shard_map/dot_general | solution.py:14
  60.3 3.3 %collective-permute-start.7 = (bf16[48,2304]{1,0:T(8,128)(2,1)S(1)}, bf16[48,2304]{1,0:T(8,128)(2,1)S(1)}, u32[]{:S(2)}, u32[]{:S(2)}) collective-permute-start(bf16[48,2304]{1,0:T(8,128)(2,1)S(1)} %fusion.89), channel_id=1, source_target_pairs={{0,6},{1,7},{2,4},{3,5},{4,2},{5,3},{6,0},{7,1},{8,14},{9,15},{10,... | collective-permute-start | bytes 663560 | tf_op jit(solution)/shard_map/ppermute | solution.py:26
  63.6 6.1 %collective-permute-done.16 = bf16[48,2304]{1,0:T(8,128)(2,1)S(1)} collective-permute-done((bf16[48,2304]{1,0:T(8,128)(2,1)S(1)}, bf16[48,2304]{1,0:T(8,128)(2,1)S(1)}, u32[]{:S(2)}, u32[]{:S(2)}) %collective-permute-start.16) | collective-permute-done | bytes 221216 | tf_op jit(solution)/shard_map/ppermute | solution.py:26
  69.7 4.2 %collective-permute-done.18 = bf16[48,2304]{1,0:T(8,128)(2,1)S(1)} collective-permute-done((bf16[48,2304]{1,0:T(8,128)(2,1)S(1)}, bf16[48,2304]{1,0:T(8,128)(2,1)S(1)}, u32[]{:S(2)}, u32[]{:S(2)}) %collective-permute-start.18) | collective-permute-done | bytes 221216 | tf_op jit(solution)/shard_map/ppermute | solution.py:26
  74.1 3.8 %collective-permute-start.19 = (bf16[48,2304]{1,0:T(8,128)(2,1)S(1)}, bf16[48,2304]{1,0:T(8,128)(2,1)S(1)}, u32[]{:S(2)}, u32[]{:S(2)}) collective-permute-start(bf16[48,2304]{1,0:T(8,128)(2,1)S(1)} %get-tuple-element.11), channel_id=1, source_target_pairs={{0,2},{1,3},{2,0},{3,1},{4,6},{5,7},{6,4},{7,5},{8,10},{9,11},{10,... | collective-permute-start | bytes 663560 | tf_op jit(solution)/shard_map/ppermute | solution.py:26
  77.9 8.8 %collective-permute-done.17 = bf16[48,2304]{1,0:T(8,128)(2,1)S(1)} collective-permute-done((bf16[48,2304]{1,0:T(8,128)(2,1)S(1)}, bf16[48,2304]{1,0:T(8,128)(2,1)S(1)}, u32[]{:S(2)}, u32[]{:S(2)}) %collective-permute-start.17) | collective-permute-done | bytes 221216 | tf_op jit(solution)/shard_map/ppermute | solution.py:26
  92.8 4.4 %collective-permute-done.21 = bf16[48,2304]{1,0:T(8,128)(2,1)S(1)} collective-permute-done((bf16[48,2304]{1,0:T(8,128)(2,1)S(1)}, bf16[48,2304]{1,0:T(8,128)(2,1)S(1)}, u32[]{:S(2)}, u32[]{:S(2)}) %collective-permute-start.21) | collective-permute-done | bytes 221216 | tf_op jit(solution)/shard_map/ppermute | solution.py:26
  98.7 8.1 %collective-permute-done.30 = bf16[48,2304]{1,0:T(8,128)(2,1)S(1)} collective-permute-done((bf16[48,2304]{1,0:T(8,128)(2,1)S(1)}, bf16[48,2304]{1,0:T(8,128)(2,1)S(1)}, u32[]{:S(2)}, u32[]{:S(2)}) %collective-permute-start.30) | collective-permute-done | bytes 221216 | tf_op jit(solution)/shard_map/ppermute | solution.py:26
  110.1 4.8 %collective-permute-done.31 = bf16[48,2304]{1,0:T(8,128)(2,1)S(1)} collective-permute-done((bf16[48,2304]{1,0:T(8,128)(2,1)S(1)}, bf16[48,2304]{1,0:T(8,128)(2,1)S(1)}, u32[]{:S(2)}, u32[]{:S(2)}) %collective-permute-start.31) | collective-permute-done | bytes 221216 | tf_op jit(solution)/shard_map/ppermute | solution.py:26
  121.9 8.7 %collective-permute-done.24 = bf16[192,1024]{1,0:T(8,128)(2,1)S(1)} collective-permute-done((bf16[192,1024]{1,0:T(8,128)(2,1)S(1)}, bf16[192,1024]{1,0:T(8,128)(2,1)S(1)}, u32[]{:S(2)}, u32[]{:S(2)}) %collective-permute-start.24) | collective-permute-done | bytes 393248 | tf_op jit(solution)/shard_map/ppermute | solution.py:50
  130.6 8.0 %collective-permute-done.33 = bf16[192,1024]{1,0:T(8,128)(2,1)S(1)} collective-permute-done((bf16[192,1024]{1,0:T(8,128)(2,1)S(1)}, bf16[192,1024]{1,0:T(8,128)(2,1)S(1)}, u32[]{:S(2)}, u32[]{:S(2)}) %collective-permute-start.33) | collective-permute-done | bytes 393248 | tf_op jit(solution)/shard_map/ppermute | solution.py:50
  152.3 6.4 %collective-permute-done.34 = bf16[48,2304]{1,0:T(8,128)(2,1)S(1)} collective-permute-done((bf16[48,2304]{1,0:T(8,128)(2,1)S(1)}, bf16[48,2304]{1,0:T(8,128)(2,1)S(1)}, u32[]{:S(2)}, u32[]{:S(2)}) %collective-permute-start.34) | collective-permute-done | bytes 221216 | tf_op jit(solution)/shard_map/ppermute | solution.py:26
  158.6 3.5 %collective-permute-done.36 = bf16[48,2304]{1,0:T(8,128)(2,1)S(1)} collective-permute-done((bf16[48,2304]{1,0:T(8,128)(2,1)S(1)}, bf16[48,2304]{1,0:T(8,128)(2,1)S(1)}, u32[]{:S(2)}, u32[]{:S(2)}) %collective-permute-start.36) | collective-permute-done | bytes 221216 | tf_op jit(solution)/shard_map/ppermute | solution.py:26
  165.9 9.0 %collective-permute-done.35 = bf16[48,2304]{1,0:T(8,128)(2,1)S(1)} collective-permute-done((bf16[48,2304]{1,0:T(8,128)(2,1)}, bf16[48,2304]{1,0:T(8,128)(2,1)S(1)}, u32[]{:S(2)}, u32[]{:S(2)}) %collective-permute-start.35) | collective-permute-done | bytes 221216 | tf_op jit(solution)/shard_map/ppermute | solution.py:26
  183.5 11.2 %collective-permute-done.43 = bf16[48,2304]{1,0:T(8,128)(2,1)S(1)} collective-permute-done((bf16[48,2304]{1,0:T(8,128)(2,1)S(1)}, bf16[48,2304]{1,0:T(8,128)(2,1)S(1)}, u32[]{:S(2)}, u32[]{:S(2)}) %collective-permute-start.43) | collective-permute-done | bytes 221216 | tf_op jit(solution)/shard_map/ppermute | solution.py:26
  198.4 7.1 %collective-permute-done.40 = bf16[48,2304]{1,0:T(8,128)(2,1)S(1)} collective-permute-done((bf16[48,2304]{1,0:T(8,128)(2,1)S(1)}, bf16[48,2304]{1,0:T(8,128)(2,1)S(1)}, u32[]{:S(2)}, u32[]{:S(2)}) %collective-permute-start.40) | collective-permute-done | bytes 221216 | tf_op jit(solution)/shard_map/ppermute | solution.py:26
  205.4 4.0 %fusion.31 = bf16[192,1024]{1,0:T(8,128)(2,1)S(1)} fusion(bf16[1024,1,2304]{2,0,1:T(8,128)(2,1)} %param.14, bf16[48,2304]{1,0:T(8,128)(2,1)S(1)} %collective-permute-done.40, bf16[48,2304]{1,0:T(8,128)(2,1)S(1)} %collective-permute-done.39, bf16[48,2304]{1,0:T(8,128)(2,1)S(1)} %collective-permute-done.38, bf16[48,2304]{1,0:T(8,128)(2,1)S(1)} %get-tuple-element.6), kind=kOutput, calls=%fused_computation.32 | convolution fusion | flops 909705216 | bytes 5996544 | tf_op jit(solution)/shard_map/dot_general | solution.py:22
  213.7 6.7 %shard_map.103 = f32[18432,128]{1,0:T(8,128)} custom-call(bf16[192,1024]{1,0:T(8,128)(2,1)S(1)} %get-tuple-element.28.c0, bf16[192,1024]{1,0:T(8,128)(2,1)S(1)} %get-tuple-element.29.c1, bf16[192,2304]{1,0:T(8,128)(2,1)S(1)} %pad_maximum_fusion.2.e0, bf16[192,2304]{1,0:T(8,128)(2,1)S(1)} %constant_dynamic-update-slice_fusion.4.e1), custom_call_target="tpu_custom_call" | custom-call | flops 1811939328 | bytes 9437184 | tf_op jit(solution)/shard_map/pallas_call | solution.py:80
  223.6 8.0 %collective-permute-done.48 = bf16[192,1024]{1,0:T(8,128)(2,1)S(1)} collective-permute-done((bf16[192,1024]{1,0:T(8,128)(2,1)S(1)}, bf16[192,1024]{1,0:T(8,128)(2,1)S(1)}, u32[]{:S(2)}, u32[]{:S(2)}) %collective-permute-start.48) | collective-permute-done | bytes 393248 | tf_op jit(solution)/shard_map/ppermute | solution.py:50
  236.5 3.1 %fusion.24 = f32[384,1024]{1,0:T(8,128)} fusion(f32[4,2,48,1024]{3,2,1,0:T(8,128)S(1)} %reverse_select_fusion, f32[2,2,2,48,1024]{4,3,2,1,0:T(8,128)S(1)} %rev.7, f32[1,2,4,48,1024]{4,3,2,1,0:T(8,128)} %rev.8, pred[]{:T(512)S(6)} %ne.10, pred[]{:T(512)S(6)} %ne.9), kind=kLoop, calls=%fused_computation.27 | loop fusion | flops 786432 | bytes 6291458 | tf_op jit(solution)/shard_map/jit(_where)/select_n | solution.py:121
  (174 shorter events, 89.0 us)
Async XLA Ops:
  0.6 16.2 %collective-permute-start.11 = (bf16[48,2304]{1,0:T(8,128)(2,1)}, bf16[48,2304]{1,0:T(8,128)(2,1)S(1)}, u32[]{:S(2)}, u32[]{:S(2)}) collective-permute-start(bf16[48,2304]{1,0:T(8,128)(2,1)} %bitcast.89), channel_id=1, source_target_pairs={{0,4},{1,5},{2,6},{3,7},{4,0},{5,1},{6,2},{7,3},{8,12},{9,13},{10,... | collective-permute-start | bytes 663560 | tf_op jit(solution)/shard_map/ppermute | solution.py:26
  4.7 17.9 %collective-permute-start.9 = (bf16[48,2304]{1,0:T(8,128)(2,1)}, bf16[48,2304]{1,0:T(8,128)(2,1)S(1)}, u32[]{:S(2)}, u32[]{:S(2)}) collective-permute-start(bf16[48,2304]{1,0:T(8,128)(2,1)} %bitcast.90), channel_id=1, source_target_pairs={{0,2},{1,3},{2,0},{3,1},{4,6},{5,7},{6,4},{7,5},{8,10},{9,11},{10,... | collective-permute-start | bytes 663560 | tf_op jit(solution)/shard_map/ppermute | solution.py:26
  6.3 16.3 %collective-permute-start.1 = (bf16[48,2304]{1,0:T(8,128)(2,1)}, bf16[48,2304]{1,0:T(8,128)(2,1)S(1)}, u32[]{:S(2)}, u32[]{:S(2)}) collective-permute-start(bf16[48,2304]{1,0:T(8,128)(2,1)} %bitcast.91), channel_id=1, source_target_pairs={{0,6},{1,7},{2,4},{3,5},{4,2},{5,3},{6,0},{7,1},{8,14},{9,15},{10,... | collective-permute-start | bytes 663560 | tf_op jit(solution)/shard_map/ppermute | solution.py:26
  6.3 32.8 %collective-permute-start = (bf16[48,2304]{1,0:T(8,128)(2,1)}, bf16[48,2304]{1,0:T(8,128)(2,1)S(1)}, u32[]{:S(2)}, u32[]{:S(2)}) collective-permute-start(bf16[48,2304]{1,0:T(8,128)(2,1)} %bitcast.92), channel_id=1, source_target_pairs={{0,1},{1,0},{2,3},{3,2},{4,5},{5,4},{6,7},{7,6},{8,9},{9,8},{10,11... | collective-permute-start | bytes 663560 | tf_op jit(solution)/shard_map/ppermute | solution.py:26
  16.9 12.9 %collective-permute-start.12 = (bf16[48,2304]{1,0:T(8,128)(2,1)S(1)}, bf16[48,2304]{1,0:T(8,128)(2,1)S(1)}, u32[]{:S(2)}, u32[]{:S(2)}) collective-permute-start(bf16[48,2304]{1,0:T(8,128)(2,1)S(1)} %collective-permute-done.11), channel_id=1, source_target_pairs={{0,1},{1,0},{2,3},{3,2},{4,5},{5,4},{6,7},{7,6},{8,9},{9,8},{10,11... | collective-permute-start | bytes 663560 | tf_op jit(solution)/shard_map/ppermute | solution.py:26
  22.6 16.5 %collective-permute-start.2 = (bf16[48,2304]{1,0:T(8,128)(2,1)S(1)}, bf16[48,2304]{1,0:T(8,128)(2,1)S(1)}, u32[]{:S(2)}, u32[]{:S(2)}) collective-permute-start(bf16[48,2304]{1,0:T(8,128)(2,1)S(1)} %collective-permute-done.1), channel_id=1, source_target_pairs={{0,1},{1,0},{2,3},{3,2},{4,5},{5,4},{6,7},{7,6},{8,9},{9,8},{10,11... | collective-permute-start | bytes 663560 | tf_op jit(solution)/shard_map/ppermute | solution.py:26
  53.5 24.4 %collective-permute-start.8 = (bf16[48,2304]{1,0:T(8,128)(2,1)S(1)}, bf16[48,2304]{1,0:T(8,128)(2,1)S(1)}, u32[]{:S(2)}, u32[]{:S(2)}) collective-permute-start(bf16[48,2304]{1,0:T(8,128)(2,1)S(1)} %get-tuple-element.17), channel_id=1, source_target_pairs={{0,1},{1,0},{2,3},{3,2},{4,5},{5,4},{6,7},{7,6},{8,9},{9,8},{10,11... | collective-permute-start | bytes 663560 | tf_op jit(solution)/shard_map/ppermute | solution.py:26
  56.5 13.2 %collective-permute-start.16 = (bf16[48,2304]{1,0:T(8,128)(2,1)S(1)}, bf16[48,2304]{1,0:T(8,128)(2,1)S(1)}, u32[]{:S(2)}, u32[]{:S(2)}) collective-permute-start(bf16[48,2304]{1,0:T(8,128)(2,1)S(1)} %get-tuple-element.18), channel_id=1, source_target_pairs={{0,1},{1,0},{2,3},{3,2},{4,5},{5,4},{6,7},{7,6},{8,9},{9,8},{10,11... | collective-permute-start | bytes 663560 | tf_op jit(solution)/shard_map/ppermute | solution.py:26
  58.1 15.8 %collective-permute-start.18 = (bf16[48,2304]{1,0:T(8,128)(2,1)S(1)}, bf16[48,2304]{1,0:T(8,128)(2,1)S(1)}, u32[]{:S(2)}, u32[]{:S(2)}) collective-permute-start(bf16[48,2304]{1,0:T(8,128)(2,1)S(1)} %get-tuple-element.19), channel_id=1, source_target_pairs={{0,1},{1,0},{2,3},{3,2},{4,5},{5,4},{6,7},{7,6},{8,9},{9,8},{10,11... | collective-permute-start | bytes 663560 | tf_op jit(solution)/shard_map/ppermute | solution.py:26
  60.3 17.6 %collective-permute-start.7 = (bf16[48,2304]{1,0:T(8,128)(2,1)S(1)}, bf16[48,2304]{1,0:T(8,128)(2,1)S(1)}, u32[]{:S(2)}, u32[]{:S(2)}) collective-permute-start(bf16[48,2304]{1,0:T(8,128)(2,1)S(1)} %fusion.89), channel_id=1, source_target_pairs={{0,6},{1,7},{2,4},{3,5},{4,2},{5,3},{6,0},{7,1},{8,14},{9,15},{10,... | collective-permute-start | bytes 663560 | tf_op jit(solution)/shard_map/ppermute | solution.py:26
  89.2 17.6 %collective-permute-start.30 = (bf16[48,2304]{1,0:T(8,128)(2,1)S(1)}, bf16[48,2304]{1,0:T(8,128)(2,1)S(1)}, u32[]{:S(2)}, u32[]{:S(2)}) collective-permute-start(bf16[48,2304]{1,0:T(8,128)(2,1)S(1)} %fusion.88), channel_id=1, source_target_pairs={{0,4},{1,5},{2,6},{3,7},{4,0},{5,1},{6,2},{7,3},{8,12},{9,13},{10,... | collective-permute-start | bytes 663560 | tf_op jit(solution)/shard_map/ppermute | solution.py:26
  89.2 19.1 %collective-permute-start.28 = (bf16[48,2304]{1,0:T(8,128)(2,1)S(1)}, bf16[48,2304]{1,0:T(8,128)(2,1)S(1)}, u32[]{:S(2)}, u32[]{:S(2)}) collective-permute-start(bf16[48,2304]{1,0:T(8,128)(2,1)S(1)} %fusion.88), channel_id=1, source_target_pairs={{0,2},{1,3},{2,0},{3,1},{4,6},{5,7},{6,4},{7,5},{8,10},{9,11},{10,... | collective-permute-start | bytes 663560 | tf_op jit(solution)/shard_map/ppermute | solution.py:26
  91.3 17.5 %collective-permute-start.20 = (bf16[48,2304]{1,0:T(8,128)(2,1)S(1)}, bf16[48,2304]{1,0:T(8,128)(2,1)S(1)}, u32[]{:S(2)}, u32[]{:S(2)}) collective-permute-start(bf16[48,2304]{1,0:T(8,128)(2,1)S(1)} %fusion.88), channel_id=1, source_target_pairs={{0,1},{1,0},{2,3},{3,2},{4,5},{5,4},{6,7},{7,6},{8,9},{9,8},{10,11... | collective-permute-start | bytes 663560 | tf_op jit(solution)/shard_map/ppermute | solution.py:26
  120.3 18.3 %collective-permute-start.33 = (bf16[192,1024]{1,0:T(8,128)(2,1)S(1)}, bf16[192,1024]{1,0:T(8,128)(2,1)S(1)}, u32[]{:S(2)}, u32[]{:S(2)}) collective-permute-start(bf16[192,1024]{1,0:T(8,128)(2,1)S(1)} %add_convert_fusion.2), channel_id=1, source_target_pairs={{0,16},{16,0},{1,17},{17,1},{2,18},{18,2},{3,19},{19,3},{4,20},{20... | collective-permute-start | bytes 1179656 | tf_op jit(solution)/shard_map/ppermute | solution.py:50
  142.3 23.6 %collective-permute-start.27 = (bf16[48,2304]{1,0:T(8,128)(2,1)}, bf16[48,2304]{1,0:T(8,128)(2,1)S(1)}, u32[]{:S(2)}, u32[]{:S(2)}) collective-permute-start(bf16[48,2304]{1,0:T(8,128)(2,1)} %get-tuple-element.13), channel_id=1, source_target_pairs={{0,1},{1,0},{2,3},{3,2},{4,5},{5,4},{6,7},{7,6},{8,9},{9,8},{10,11... | collective-permute-start | bytes 663560 | tf_op jit(solution)/shard_map/ppermute | solution.py:26
  144.0 14.6 %collective-permute-start.34 = (bf16[48,2304]{1,0:T(8,128)(2,1)S(1)}, bf16[48,2304]{1,0:T(8,128)(2,1)S(1)}, u32[]{:S(2)}, u32[]{:S(2)}) collective-permute-start(bf16[48,2304]{1,0:T(8,128)(2,1)S(1)} %get-tuple-element.14), channel_id=1, source_target_pairs={{0,1},{1,0},{2,3},{3,2},{4,5},{5,4},{6,7},{7,6},{8,9},{9,8},{10,11... | collective-permute-start | bytes 663560 | tf_op jit(solution)/shard_map/ppermute | solution.py:26
  145.6 16.5 %collective-permute-start.36 = (bf16[48,2304]{1,0:T(8,128)(2,1)S(1)}, bf16[48,2304]{1,0:T(8,128)(2,1)S(1)}, u32[]{:S(2)}, u32[]{:S(2)}) collective-permute-start(bf16[48,2304]{1,0:T(8,128)(2,1)S(1)} %get-tuple-element.15), channel_id=1, source_target_pairs={{0,1},{1,0},{2,3},{3,2},{4,5},{5,4},{6,7},{7,6},{8,9},{9,8},{10,11... | collective-permute-start | bytes 663560 | tf_op jit(solution)/shard_map/ppermute | solution.py:26
  149.9 16.0 %collective-permute-start.26 = (bf16[48,2304]{1,0:T(8,128)(2,1)}, bf16[48,2304]{1,0:T(8,128)(2,1)S(1)}, u32[]{:S(2)}, u32[]{:S(2)}) collective-permute-start(bf16[48,2304]{1,0:T(8,128)(2,1)} %fusion.82), channel_id=1, source_target_pairs={{0,6},{1,7},{2,4},{3,5},{4,2},{5,3},{6,0},{7,1},{8,14},{9,15},{10,... | collective-permute-start | bytes 663560 | tf_op jit(solution)/shard_map/ppermute | solution.py:26
  177.6 17.1 %collective-permute-start.43 = (bf16[48,2304]{1,0:T(8,128)(2,1)S(1)}, bf16[48,2304]{1,0:T(8,128)(2,1)S(1)}, u32[]{:S(2)}, u32[]{:S(2)}) collective-permute-start(bf16[48,2304]{1,0:T(8,128)(2,1)S(1)} %get-tuple-element.6), channel_id=1, source_target_pairs={{0,4},{1,5},{2,6},{3,7},{4,0},{5,1},{6,2},{7,3},{8,12},{9,13},{10,... | collective-permute-start | bytes 663560 | tf_op jit(solution)/shard_map/ppermute | solution.py:26
  179.0 17.3 %collective-permute-start.41 = (bf16[48,2304]{1,0:T(8,128)(2,1)S(1)}, bf16[48,2304]{1,0:T(8,128)(2,1)S(1)}, u32[]{:S(2)}, u32[]{:S(2)}) collective-permute-start(bf16[48,2304]{1,0:T(8,128)(2,1)S(1)} %get-tuple-element.6), channel_id=1, source_target_pairs={{0,2},{1,3},{2,0},{3,1},{4,6},{5,7},{6,4},{7,5},{8,10},{9,11},{10,... | collective-permute-start | bytes 663560 | tf_op jit(solution)/shard_map/ppermute | solution.py:26
  180.6 16.1 %collective-permute-start.39 = (bf16[48,2304]{1,0:T(8,128)(2,1)S(1)}, bf16[48,2304]{1,0:T(8,128)(2,1)S(1)}, u32[]{:S(2)}, u32[]{:S(2)}) collective-permute-start(bf16[48,2304]{1,0:T(8,128)(2,1)S(1)} %get-tuple-element.6), channel_id=1, source_target_pairs={{0,6},{1,7},{2,4},{3,5},{4,2},{5,3},{6,0},{7,1},{8,14},{9,15},{10,... | collective-permute-start | bytes 663560 | tf_op jit(solution)/shard_map/ppermute | solution.py:26
  182.0 16.3 %collective-permute-start.38 = (bf16[48,2304]{1,0:T(8,128)(2,1)S(1)}, bf16[48,2304]{1,0:T(8,128)(2,1)S(1)}, u32[]{:S(2)}, u32[]{:S(2)}) collective-permute-start(bf16[48,2304]{1,0:T(8,128)(2,1)S(1)} %get-tuple-element.6), channel_id=1, source_target_pairs={{0,1},{1,0},{2,3},{3,2},{4,5},{5,4},{6,7},{7,6},{8,9},{9,8},{10,11... | collective-permute-start | bytes 663560 | tf_op jit(solution)/shard_map/ppermute | solution.py:26
  194.8 14.8 %collective-permute-start.44 = (bf16[48,2304]{1,0:T(8,128)(2,1)S(1)}, bf16[48,2304]{1,0:T(8,128)(2,1)S(1)}, u32[]{:S(2)}, u32[]{:S(2)}) collective-permute-start(bf16[48,2304]{1,0:T(8,128)(2,1)S(1)} %collective-permute-done.43), channel_id=1, source_target_pairs={{0,1},{1,0},{2,3},{3,2},{4,5},{5,4},{6,7},{7,6},{8,9},{9,8},{10,11... | collective-permute-start | bytes 663560 | tf_op jit(solution)/shard_map/ppermute | solution.py:26
  196.3 13.2 %collective-permute-start.42 = (bf16[48,2304]{1,0:T(8,128)(2,1)S(1)}, bf16[48,2304]{1,0:T(8,128)(2,1)S(1)}, u32[]{:S(2)}, u32[]{:S(2)}) collective-permute-start(bf16[48,2304]{1,0:T(8,128)(2,1)S(1)} %collective-permute-done.41), channel_id=1, source_target_pairs={{0,1},{1,0},{2,3},{3,2},{4,5},{5,4},{6,7},{7,6},{8,9},{9,8},{10,11... | collective-permute-start | bytes 663560 | tf_op jit(solution)/shard_map/ppermute | solution.py:26
  (44 other events, 489.2 us)

commit v2 on v0

--- a/solution.py
+++ b/solution.py
@@ -1,22 +1,393 @@
 import jax
 import jax.numpy as jnp
 from jax import lax
+from jax.experimental import pallas as pl
+from jax.experimental.pallas import tpu as pltpu
 from jax.sharding import PartitionSpec as P
 
+F32, BF16 = jnp.float32, jnp.bfloat16
+SWAP2 = [(0, 1), (1, 0)]
+LARGE = pl.CostEstimate(flops=20_000_000_000, bytes_accessed=1000, transcendentals=0)
+MEDIUM = pl.CostEstimate(flops=1_200_000_000, bytes_accessed=1000, transcendentals=0)
+SMALL = pl.CostEstimate(flops=1000, bytes_accessed=1000, transcendentals=0)
+
 
 def contract_rows(left, right):
-    return lax.dot_general(
-        left, right, (((0,), (0,)), ((), ())), preferred_element_type=jnp.float32
+    return lax.dot_general(left, right, (((0,), (0,)), ((), ())), preferred_element_type=F32)
+
+
+def contract_cols(left, right):
+    return lax.dot_general(left, right, (((1,), (1,)), ((), ())), preferred_element_type=F32)
+
+
+def dot(a, b):
+    return jnp.dot(a, b, preferred_element_type=F32)
+
+
+def after(x, *first):
+    return lax.optimization_barrier((x,) + first)[0]
+
+
+def swap(x, k):
+    return lax.ppermute(x, "lat", [(i, i ^ k) for i in range(8)])
+
+
+def pair(x, axis):
+    return lax.ppermute(x, axis, SWAP2)
+
+
+def gather(x, first=(), mid=(), weight=None):
+    z1, y0, z3, z2 = swap(x, 2), swap(x, 1), swap(x, 6), swap(x, 4)
+    y1 = swap(after(z1, y0), 1)
+    y3 = swap(after(z3, *first), 1)
+    if weight is not None:
+        weight = load_after(weight, z3)
+        mid = (weight,)
+    y2 = swap(after(z2, *mid), 1)
+    return (after(x, y1, z2), y0, z3, y3), (z1, y1, z2, y2), weight
+
+
+def call(kernel, grid, in_specs, out_specs, out_shape, scratch=(), mib=24):
+    return pl.pallas_call(
+        kernel,
+        grid=grid,
+        in_specs=in_specs,
+        out_specs=out_specs,
+        out_shape=out_shape,
+        scratch_shapes=scratch,
+        compiler_params=pltpu.CompilerParams(vmem_limit_bytes=mib << 20),
+        cost_estimate=LARGE,
     )
 
 
-def contract_cols(left, right):
-    return lax.dot_general(
-        left, right, (((1,), (1,)), ((), ())), preferred_element_type=jnp.float32
-    )
+def whole(x):
+    return pl.BlockSpec(x.shape, lambda i: (0,) * x.ndim)
+
+
+def fast(shape, dtype):
+    return pltpu.VMEM(tuple(shape), dtype)
+
+
+def in_vmem(x):
+    return pltpu.with_memory_space_constraint(x, pltpu.VMEM)
+
+
+def vmem_call(kernel, args, out_shape, scratch=(), mib=8, cost=SMALL, scalar=None, first=()):
+    spec = pl.BlockSpec(memory_space=pltpu.VMEM)
+    n = len(out_shape) if isinstance(out_shape, (list, tuple)) else 0
+    scalars = [] if scalar is None else [scalar]
+    k = len(first)
+
+    return pl.pallas_call(
+        lambda *refs: kernel(*refs[k:]),
+        in_specs=[pl.BlockSpec(memory_space=pl.ANY)] * k
+        + [pl.BlockSpec(memory_space=pltpu.SMEM)] * len(scalars) + [spec] * len(args),
+        out_specs=[spec] * n if n else spec,
+        out_shape=out_shape,
+        scratch_shapes=scratch,
+        compiler_params=pltpu.CompilerParams(vmem_limit_bytes=mib << 20),
+        cost_estimate=cost,
+    )(*first, *scalars, *[in_vmem(a) for a in args])
+
+
+def load_kernel(src, dst, sem):
+    c = pltpu.make_async_copy(src, dst, sem)
+    c.start()
+    c.wait()
+
+
+def load(w, *first):
+    w = after(w, *first) if first else w
+    return pl.pallas_call(
+        load_kernel,
+        in_specs=[pl.BlockSpec(memory_space=pltpu.HBM)],
+        out_specs=pl.BlockSpec(memory_space=pltpu.VMEM),
+        out_shape=fast(w.shape, w.dtype),
+        scratch_shapes=[pltpu.SemaphoreType.DMA],
+        compiler_params=pltpu.CompilerParams(vmem_limit_bytes=1 << 20),
+        cost_estimate=SMALL,
+    )(pltpu.with_memory_space_constraint(w, pltpu.HBM))
+
+
+def load_after(w, first):
+    def kernel(_, src, dst, sem):
+        load_kernel(src, dst, sem)
+
+    return pl.pallas_call(
+        kernel,
+        in_specs=[pl.BlockSpec(memory_space=pl.ANY), pl.BlockSpec(memory_space=pltpu.HBM)],
+        out_specs=pl.BlockSpec(memory_space=pltpu.VMEM),
+        out_shape=fast(w.shape, w.dtype),
+        scratch_shapes=[pltpu.SemaphoreType.DMA],
+        compiler_params=pltpu.CompilerParams(vmem_limit_bytes=1 << 20),
+        cost_estimate=SMALL,
+    )(first, pltpu.with_memory_space_constraint(w, pltpu.HBM))
+
+
+def assemble(blocks, xs):
+    r = blocks[0].shape[0]
+    for k, b in enumerate(blocks):
+        xs[k * r:(k + 1) * r, :] = b[...]
+
+
+def tiles(n, w, step):
+    w = next(k for k in (768, 512, w) if n % k == 0)
+
+    def run(i, _):
+        step(pl.ds(pl.multiple_of(i * w, w), w))
+        return 0
+
+    lax.fori_loop(0, n // w, run, 0)
+
+
+def gate_up_kernel(b0, b1, b2, b3, gate, up, out, xs):
+    assemble((b0, b1, b2, b3), xs)
+
+    def step(cols):
+        out[0, :, cols] = dot(xs[...], gate[:, cols]).astype(BF16)
+        out[1, :, cols] = dot(xs[...], up[:, cols]).astype(BF16)
+
+    tiles(gate.shape[1], 256, step)
+
+
+def gate_up(blocks, gate, up):
+    r, d = blocks[0].shape
+    return vmem_call(gate_up_kernel, (*blocks, gate, up), fast((2, 4 * r, gate.shape[1]), BF16),
+                     [pltpu.VMEM((4 * r, d), BF16)])
+
+
+def store_parts(p, r, cols, keep, send0, send1):
+    keep[0, :, cols] = p[:r]
+    send0[:, cols] = p[r:2 * r].astype(BF16)
+    keep[1, :, cols] = p[2 * r:3 * r]
+    send1[:, cols] = p[3 * r:].astype(BF16)
+
+
+def down_kernel(own, got, weight, keep, send0, send1, hid):
+    def act(cols):
+        v = own[:, :, cols].astype(F32) + got[:, :, cols].astype(F32)
+        hid[:, cols] = (jax.nn.gelu(v[0], approximate=True) * v[1]).astype(BF16)
+
+    tiles(hid.shape[1], 256, act)
+
+    def step(cols):
+        store_parts(dot(hid[...], weight[:, cols]), keep.shape[1], cols, keep, send0, send1)
+
+    tiles(weight.shape[1], 256, step)
+
+
+def parts_shapes(r, d):
+    return [fast((2, r, d), F32)] + [fast((r, d), BF16)] * 2
+
+
+def down(own, got, weight):
+    _, m, n = own.shape
+    return vmem_call(down_kernel, (own, got, weight), parts_shapes(m // 4, weight.shape[1]),
+                     [pltpu.VMEM((m, n), BF16)])
+
+
+def assemble_halves(tok, blocks, xs):
+    r = blocks[0].shape[0]
+    for k, b in enumerate(blocks):
+        row = pl.multiple_of(((k // 2) ^ tok) * (2 * r) + (k % 2) * r, r)
+        xs[pl.ds(row, r), :] = b[...]
+
+
+def store_halves(p, cols, mine, away):
+    h = mine.shape[0]
+    mine[:, cols] = p[:h].astype(BF16)
+    away[:, cols] = p[h:].astype(BF16)
+
+
+def encode_kernel(tok, b0, b1, b2, b3, weight, mine, away, xs):
+    assemble_halves(tok[0], (b0, b1, b2, b3), xs)
+
+    def step(cols):
+        store_halves(dot(xs[...], weight[:, cols]), cols, mine, away)
+
+    tiles(weight.shape[1], 256, step)
+
+
+def encode(tok, blocks, weight, cost=SMALL):
+    r, d = blocks[0].shape
+    return vmem_call(encode_kernel, (*blocks, weight), [fast((2 * r, weight.shape[1]), BF16)] * 2,
+                     [pltpu.VMEM((4 * r, d), BF16)], cost=cost, scalar=tok)
+
+
+def decode_kernel(tok, own0, got0, own1, got1, weight, codes0, codes1, *parts):
+    h = own0.shape[0]
+    for codes, own, got in ((codes0, own0, got0), (codes1, own1, got1)):
+        codes[pl.ds(pl.multiple_of(tok[0] * h, h), h), :] = own[...]
+        codes[pl.ds(pl.multiple_of((1 - tok[0]) * h, h), h), :] = got[...]
+
+    def step(cols):
+        w = weight[:, cols]
+        for codes, out in ((codes0, parts[:3]), (codes1, parts[3:])):
+            store_parts(dot(codes[...], w), h // 2, cols, *out)
+
+    tiles(weight.shape[1], 256, step)
+
+
+def decode(tok, own0, got0, own1, got1, weight):
+    h, n = own0.shape
+    return vmem_call(decode_kernel, (own0, got0, own1, got1, weight),
+                     [fast((2 * h, n), BF16)] * 2 + parts_shapes(h // 2, weight.shape[1]) * 2, scalar=tok)
+
+
+def latent_kernel(tok, b0, b1, b2, b3, weight, mine, away, xs):
+    assemble_halves(tok[0], (b0, b1, b2, b3), xs)
+
+    def step(cols):
+        store_halves(contract_cols(xs[...], weight[cols, :]), cols, mine, away)
+
+    tiles(weight.shape[0], 256, step)
+
+
+def latent(tok, blocks, weight, cost=SMALL):
+    r, d = blocks[0].shape
+    return vmem_call(latent_kernel, (*blocks, weight), [fast((2 * r, weight.shape[0]), BF16)] * 2,
+                     [pltpu.VMEM((4 * r, d), BF16)], cost=cost, scalar=tok)
+
+
+def grid_assemble(blocks, xs):
+    @pl.when(pl.program_id(0) == 0)
+    def _():
+        assemble(blocks, xs)
+
+
+def grad_kernel(c0, c1, *refs):
+    blocks, out, mark, es = refs[:8], refs[9], refs[10], refs[11]
+    mark[...] = jnp.zeros_like(mark)
+    grid_assemble(blocks, es)
+    n, w = c0.shape[1], es.shape[1]
+    m = c0.shape[0]
+    cols = w // 128
+    r = contract_rows(c0[...], es[:m]) + contract_rows(c1[...], es[m:])
+    for c in range(cols):
+        out[pl.ds(c, n, cols), :] = r[:, c * 128:(c + 1) * 128]
+
+
+def decoder_grad(codes, blocks, first):
+    m, n = codes[0].shape
+    r, w = blocks[0].shape
+    step = 256
+    cspec = pl.BlockSpec((m, step), lambda i: (0, i))
+    out, mark = call(
+        grad_kernel, (n // step,),
+        [cspec, cspec] + [whole(blocks[0])] * 8 + [pl.BlockSpec(memory_space=pl.ANY)],
+        [pl.BlockSpec((step * w // 128, 128), lambda i: (i, 0)), pl.BlockSpec((8, 128), lambda i: (0, 0))],
+        [jax.ShapeDtypeStruct((n * w // 128, 128), F32), jax.ShapeDtypeStruct((8, 128), F32)],
+        [pltpu.VMEM((8 * r, w), BF16)],
+    )(*codes, *blocks, first)
+    return out.reshape(n, 1, w), mark
+
+
+def order_kernel(who, a0, g0, a1, g1, out, sems):
+    r = a0.shape[0] // 2
+    for i in range(8):
+        k = i ^ who[0]
+        row = pl.multiple_of((k & 1) * r, r)
+        second = (k >= 2) & (k < 6)
+        mine = jnp.where(k >= 4, 1, 0) == who[1]
+        for ref, here in ((a0, mine & ~second), (g0, ~mine & ~second), (a1, mine & second), (g1, ~mine & second)):
+            @pl.when(here)
+            def _():
+                pltpu.make_async_copy(ref.at[pl.ds(row, r)], out.at[pl.ds(i * r, r)], sems.at[i]).start()
+    for i in range(8):
+        pltpu.make_async_copy(a0.at[pl.ds(0, r)], out.at[pl.ds(i * r, r)], sems.at[i]).wait()
+
+
+def ordered(who, a0, g0, a1, g1):
+    h, n = a0.shape
+    spec = pl.BlockSpec(memory_space=pltpu.VMEM)
+    return pl.pallas_call(
+        order_kernel,
+        in_specs=[pl.BlockSpec(memory_space=pltpu.SMEM)] + [spec] * 4,
+        out_specs=pl.BlockSpec(memory_space=pl.ANY),
+        out_shape=jax.ShapeDtypeStruct((4 * h, n), F32),
+        scratch_shapes=[pltpu.SemaphoreType.DMA((8,))],
+        compiler_params=pltpu.CompilerParams(vmem_limit_bytes=4 << 20),
+        cost_estimate=SMALL,
+    )(who, in_vmem(a0), in_vmem(g0), in_vmem(a1), in_vmem(g1))
+
+
+def plus(mine, got):
+    return mine + got.astype(F32)
+
+
+def scatter(a, b):
+    keep, send0, send3 = a
+    got3 = swap(send3, 1)
+    s3 = swap(plus(keep[1], got3).astype(BF16), 6)
+    keep0, (keep, send1, send2) = keep[0], b
+    got2 = swap(after(send2, got3), 1)
+    got1 = swap(after(send1, got2), 1)
+    s = plus(plus(keep0, swap(after(send0, got1), 1)), s3)
+    t2 = plus(keep[1], got2).astype(BF16)
+    s2 = swap(t2, 4)
+    s1 = swap(plus(keep[0], after(got1, t2)).astype(BF16), 2)
+    return plus(add(s, s2, MEDIUM), s1)
+
+
+def add_kernel(a, b, out):
+    out[...] = a[...].astype(F32) + b[...].astype(F32)
+
+
+def add(a, b, cost=SMALL, first=()):
+    return vmem_call(add_kernel, (a, b), fast(a.shape, F32), cost=cost, first=first)
+
+
+def chip_sum(mine, away):
+    return plus(mine.astype(F32), pair(away, "tok")).astype(BF16)
+
+
+def code_kernel(q, m, bias, out):
+    out[...] = jnp.maximum(q[...].astype(F32) + m[...].astype(F32) + bias[...], 0.0).astype(BF16)
+
+
+def to_codes(q, bias):
+    return vmem_call(code_kernel, (q, pair(q, "mp"), bias), fast(q.shape, BF16))
 
 
 def body(inputs, gate_w, up_w, down_w, enc_w, enc_bias, dec_w, dec_bias):
+    me = lax.axis_index("lat")
+    tok = lax.axis_index("tok").reshape(1)
+    gate_l, up_l, down_l, enc_l = gate_w[0], up_w[0], down_w[0], enc_w[0]
+    dec_l = dec_w[:, 0, :]
+    bias = enc_bias[None]
+    gate_l = load(gate_l)
+    up_l = load(up_l, gate_l)
+    down_l = load(down_l, up_l)
+    xa, xb, _ = gather(inputs[0], (up_l,), (down_l,))
+    gl = after(gate_l, down_l)
+    ga = gate_up(xa, gl, up_l)
+    gb = gate_up((after(xb[0], ga),) + xb[1:], gate_l, up_l)
+    pa = down(ga, pair(ga, "tok"), after(down_l, gb))
+    pb = down(gb, pair(gb, "tok"), after(down_l, pa[0]))
+    acts = scatter(pa, pb).astype(BF16)
+
+    aa, ab, enc_2 = gather(acts, weight=enc_l)
+    qa = chip_sum(*encode(tok, aa, enc_2))
+    ha = to_codes(qa, bias)
+    mine, away = encode(tok, (after(ab[0], qa),) + ab[1:], enc_2)
+    halves = [ha, to_codes(chip_sum(after(mine, ha), away), bias)]
+    joined = [c for h in halves for c in (h, pair(h, "tok"))]
+    ca, cb, *r = decode(tok, *joined, dec_l)
+    err = scatter(r[:3], r[3:]) + dec_bias[0] - acts.astype(F32)
+
+    ea, eb, _ = gather(err.astype(BF16))
+    dec_3 = load_after(dec_l, eb[2])
+    mine, away = latent(tok, ea, dec_3)
+    la = chip_sum(after(mine, eb[3]), away)
+    lb = chip_sum(*latent(tok, (after(eb[0], la),) + eb[1:], dec_3))
+    dec_grad, t = decoder_grad((ca, cb), ea + eb, lb)
+    la, lb = [add(l, pair(l, "mp"), first=(t,)) for l in (la, lb)]
+    who = jnp.concatenate([me.reshape(1), tok])
+    lat = ordered(who, la, pair(la, "tok"), lb, pair(lb, "tok"))
+    return (err[None], dec_grad, lat)
+
+
+def plain_body(inputs, gate_w, up_w, down_w, enc_w, enc_bias, dec_w, dec_bias):
     x_rows = inputs[0]
     gathered = lax.all_gather(x_rows, "lat", axis=0, tiled=True)
     gate_local = gate_w[0]
@@ -66,6 +437,8 @@
 
 
 def solution(mesh):
+    sizes = [mesh.shape[a] for a in ("mp", "tok", "lat")]
+    step = body if sizes == [2, 2, 8] else plain_body
     in_specs = (
         P("mp", "lat", "tok"),
         P("mp", "tok", "lat"),
@@ -77,4 +450,4 @@
         P("mp", "tok"),
     )
     out_specs = (P("mp", "lat", "tok"), P("lat", "mp", "tok"), P(None, "lat"))
-    return jax.shard_map(body, mesh=mesh, in_specs=in_specs, out_specs=out_specs, check_vma=False)
+    return jax.shard_map(step, mesh=mesh, in_specs=in_specs, out_specs=out_specs, check_vma=False)

time: 503 us -> 201 us (0.40)
  waiting for transfers between devices: 372 us -> 81.8 us
  starting transfers between devices: 0.55 us -> 64.8 us
  local copies, waits for them, and re-layouts: 57 us -> 0.03 us
  Pallas kernels: 0 us -> 50.6 us
  matrix products: 48.9 us -> 0 us
  between operations: 13.9 us -> 1.01 us
  other arithmetic: 11.1 us -> 2.56 us
    reduce_scatter x3 -> x0, waiting for transfers between devices: 174 us -> none  [the longest x1 80.4 us: body(): lax.psum_scatter(jnp.dot(block, down_local, preferred_element_type=jnp.fl...]
    all_gather x4 -> x0, waiting for transfers between devices: 155 us -> none  [the longest x1 50.9 us: body(): gathered = lax.all_gather(x_rows, 'lat', axis=0, tiled=True)]
    ppermute x0 -> x49, waiting for transfers between devices: none -> 81.8 us  [the longest x35 67.9 us: swap(): return lax.ppermute(x, 'lat', [(i, i ^ k) for i in range(8)])]
    ppermute x0 -> x49, starting transfers between devices: none -> 64.8 us  [the longest x35 58.1 us: swap(): return lax.ppermute(x, 'lat', [(i, i ^ k) for i in range(8)])]
    unnamed x14 -> x10, local copies, waits for them, and re-layouts: 57 us -> 0.03 us
    pallas_call x0 -> x22, Pallas kernels: none -> 50.6 us  [the longest x15 26.5 us: vmem_call(): pl.pallas_call(lambda *refs: kernel(*refs[k:]), in_specs=[pl.BlockSpec(me...]
    dot_general x7 -> x0, matrix products: 48.9 us -> none  [the longest x1 10.6 us: body(): jnp.dot(block, down_local, preferred_element_type=jnp.float32)]
    psum x2 -> x0, waiting for transfers between devices: 42 us -> none  [the longest x1 42 us: body(): pre = lax.psum(partial_pre, ('mp', 'tok'))]
  transfers between devices with their start and end apart: 9 -> 49, of which waited for: 8 -> 30; matrix products, arithmetic and copies ran while one was open for 11% -> 1% of each run, Pallas kernels for 0% -> 21%
where the time goes in v2:
time: 201 us
  waiting for transfers between devices  81.8 us (41%)
  starting transfers between devices  64.8 us (32%)
  Pallas kernels  50.6 us (25%)
  other arithmetic  2.56 us (1%)
    ppermute x35, waiting for transfers between devices, swap(): return lax.ppermute(x, 'lat', [(i, i ^ k) for i in range(8)])  67.9 us
    ppermute x35, starting transfers between devices, swap(): return lax.ppermute(x, 'lat', [(i, i ^ k) for i in range(8)])  58.1 us
    pallas_call x15, Pallas kernels, vmem_call(): pl.pallas_call(lambda *refs: kernel(*refs[k:]), in_specs=[pl.BlockSpec(me...  26.5 us
    ppermute x14, waiting for transfers between devices, pair(): return lax.ppermute(x, axis, SWAP2)  13.9 us
    pallas_call x3, Pallas kernels, load(): pl.pallas_call(load_kernel, in_specs=[pl.BlockSpec(memory_space=pltpu.HBM...  12.1 us
    ppermute x14, starting transfers between devices, pair(): return lax.ppermute(x, axis, SWAP2)  6.79 us
    pallas_call x1, Pallas kernels, decoder_grad(): call(grad_kernel, (n // step,), [cspec, cspec] + [whole(blocks[0])] * 8 +...  5.45 us
    pallas_call x2, Pallas kernels, load_after(): pl.pallas_call(kernel, in_specs=[pl.BlockSpec(memory_space=pl.ANY), pl.Bl...  4.84 us
  transfers between devices with their start and end apart: 49, of which 30 were waited for; matrix products, arithmetic and copies ran while one was open for 1% of the time, Pallas kernels for 21%

profile of v2, /device:TPU:0, one launch (start us, length us, event | category | flops | bytes accessed | tf_op | source)
XLA Modules:
  0.0 200.9 jit_solution(15191614008631534412)
XLA Ops:
  7.8 4.0 %shard_map.103.refs_4_ = bf16[2304,2304]{1,0:T(8,128)(2,1)S(1)} custom-call(bf16[2304,2304]{1,0:T(8,128)(2,1)} %bitcast.55), custom_call_target="tpu_custom_call" | custom-call | flops 1000 | bytes 1000 | tf_op jit(solution)/shard_map/pallas_call | solution.py:101
  11.9 4.0 %shard_map.104.refs_5_ = bf16[2304,2304]{1,0:T(8,128)(2,1)S(1)} custom-call(bf16[2304,2304]{1,0:T(8,128)(2,1)} %bitcast.56), custom_call_target="tpu_custom_call" | custom-call | flops 1000 | bytes 1000 | tf_op jit(solution)/shard_map/pallas_call | solution.py:101
  19.1 4.1 %shard_map.105.refs_2_ = bf16[2304,2304]{1,0:T(8,128)(2,1)S(1)} custom-call(bf16[2304,2304]{1,0:T(8,128)(2,1)} %bitcast.57), custom_call_target="tpu_custom_call" | custom-call | flops 1000 | bytes 1000 | tf_op jit(solution)/shard_map/pallas_call | solution.py:101
  23.1 4.0 %collective-permute-done.3.refs_2_ = bf16[48,2304]{1,0:T(8,128)(2,1)S(1)} collective-permute-done((bf16[48,2304]{1,0:T(8,128)(2,1)}, bf16[48,2304]{1,0:T(8,128)(2,1)S(1)}, u32[]{:S(2)}, u32[]{:S(2)}) %collective-permute-start.3) | collective-permute-done | bytes 221216 | tf_op jit(solution)/shard_map/ppermute | solution.py:32
  27.7 4.7 %shard_map.106.refs_0_ = bf16[2,192,2304]{2,1,0:T(8,128)(2,1)S(1)} custom-call(bf16[48,2304]{1,0:T(8,128)(2,1)S(1)} %bitcast.52, bf16[48,2304]{1,0:T(8,128)(2,1)S(1)} %collective-permute-done.1.refs_1_, bf16[48,2304]{1,0:T(8,128)(2,1)S(1)} %collective-permute-done.4.refs_2_, bf16[48,2304]{1,0:T(8,128)(2,1)S(1)} %collective-permute-done.5.refs_3_, ...), custom_call_target="tpu_custom_call" | custom-call | flops 1000 | bytes 1000 | tf_op jit(solution)/shard_map/pallas_call | solution.py:81
  33.1 4.7 %shard_map.107.refs_0_ = bf16[2,192,2304]{2,1,0:T(8,128)(2,1)S(1)} custom-call(bf16[48,2304]{1,0:T(8,128)(2,1)S(1)} %collective-permute-done.refs_0_, bf16[48,2304]{1,0:T(8,128)(2,1)S(1)} %collective-permute-done.2.refs_1_, bf16[48,2304]{1,0:T(8,128)(2,1)S(1)} %collective-permute-done.3.refs_2_, bf16[48,2304]{1,0:T(8,128)(2,1)S(1)} %collective-permute-done.7.refs_3_, ...), custom_call_target="tpu_custom_call" | custom-call | flops 1000 | bytes 1000 | tf_op jit(solution)/shard_map/pallas_call | solution.py:81
  38.0 3.6 %shard_map.108 = (f32[2,48,2304]{2,1,0:T(8,128)S(1)}, bf16[48,2304]{1,0:T(8,128)(2,1)S(1)}, bf16[48,2304]{1,0:T(8,128)(2,1)S(1)}) custom-call(bf16[2,192,2304]{2,1,0:T(8,128)(2,1)S(1)} %shard_map.106.refs_0_, bf16[2,192,2304]{2,1,0:T(8,128)(2,1)S(1)} %collective-permute-done.6.refs_1_, bf16[2304,2304]{1,0:T(8,128)(2,1)S(1)} %shard_map.105.refs_2_), custom_call_target="tpu_custom_call" | custom-call | flops 1000 | bytes 1000 | tf_op jit(solution)/shard_map/pallas_call | solution.py:81
  43.0 3.6 %shard_map.109 = (f32[2,48,2304]{2,1,0:T(8,128)S(1)}, bf16[48,2304]{1,0:T(8,128)(2,1)S(1)}, bf16[48,2304]{1,0:T(8,128)(2,1)S(1)}) custom-call(bf16[2,192,2304]{2,1,0:T(8,128)(2,1)S(1)} %shard_map.107.refs_0_, bf16[2,192,2304]{2,1,0:T(8,128)(2,1)S(1)} %collective-permute-done.8.refs_1_, bf16[2304,2304]{1,0:T(8,128)(2,1)S(1)} %shard_map.105.refs_2_), custom_call_target="tpu_custom_call" | custom-call | flops 1000 | bytes 1000 | tf_op jit(solution)/shard_map/pallas_call | solution.py:81
  53.1 3.4 %collective-permute-done.10 = bf16[48,2304]{1,0:T(8,128)(2,1)S(1)} collective-permute-done((bf16[48,2304]{1,0:T(8,128)(2,1)S(1)}, bf16[48,2304]{1,0:T(8,128)(2,1)S(1)}, u32[]{:S(2)}, u32[]{:S(2)}) %collective-permute-start.10) | collective-permute-done | bytes 221216 | tf_op jit(solution)/shard_map/ppermute | solution.py:32
  56.9 4.8 %collective-permute-start.14 = (bf16[48,2304]{1,0:T(8,128)(2,1)S(1)}, bf16[48,2304]{1,0:T(8,128)(2,1)S(1)}, u32[]{:S(2)}, u32[]{:S(2)}) collective-permute-start(bf16[48,2304]{1,0:T(8,128)(2,1)S(1)} %fusion.5), channel_id=1, source_target_pairs={{0,4},{1,5},{2,6},{3,7},{4,0},{5,1},{6,2},{7,3},{8,12},{9,13},{10,... | collective-permute-start | bytes 663560 | tf_op jit(solution)/shard_map/ppermute | solution.py:32
  63.2 3.6 %collective-permute-start.15 = (bf16[48,2304]{1,0:T(8,128)(2,1)S(1)}, bf16[48,2304]{1,0:T(8,128)(2,1)S(1)}, u32[]{:S(2)}, u32[]{:S(2)}) collective-permute-start(bf16[48,2304]{1,0:T(8,128)(2,1)S(1)} %fusion.4), channel_id=1, source_target_pairs={{0,2},{1,3},{2,0},{3,1},{4,6},{5,7},{6,4},{7,5},{8,10},{9,11},{10,... | collective-permute-start | bytes 663560 | tf_op jit(solution)/shard_map/ppermute | solution.py:32
  68.6 4.2 %collective-permute-done.14.refs_1_ = bf16[48,2304]{1,0:T(8,128)(2,1)S(1)} collective-permute-done((bf16[48,2304]{1,0:T(8,128)(2,1)S(1)}, bf16[48,2304]{1,0:T(8,128)(2,1)S(1)}, u32[]{:S(2)}, u32[]{:S(2)}) %collective-permute-start.14) | collective-permute-done | bytes 221216 | tf_op jit(solution)/shard_map/ppermute | solution.py:32
  80.3 3.2 %collective-permute-done.16.refs_1_ = bf16[48,2304]{1,0:T(8,128)(2,1)S(1)} collective-permute-done((bf16[48,2304]{1,0:T(8,128)(2,1)S(1)}, bf16[48,2304]{1,0:T(8,128)(2,1)S(1)}, u32[]{:S(2)}, u32[]{:S(2)}) %collective-permute-start.16) | collective-permute-done | bytes 221216 | tf_op jit(solution)/shard_map/ppermute | solution.py:32
  83.5 3.5 %collective-permute-start.18 = (bf16[48,2304]{1,0:T(8,128)(2,1)S(1)}, bf16[48,2304]{1,0:T(8,128)(2,1)S(1)}, u32[]{:S(2)}, u32[]{:S(2)}) collective-permute-start(bf16[48,2304]{1,0:T(8,128)(2,1)S(1)} %collective-permute-done.16.refs_1_), channel_id=1, source_target_pairs={{0,1},{1,0},{2,3},{3,2},{4,5},{5,4},{6,7},{7,6},{8,9},{9,8},{10,11... | collective-permute-start | bytes 663560 | tf_op jit(solution)/shard_map/ppermute | solution.py:32
  92.5 4.6 %collective-permute-done.19.refs_3_ = bf16[48,2304]{1,0:T(8,128)(2,1)S(1)} collective-permute-done((bf16[48,2304]{1,0:T(8,128)(2,1)S(1)}, bf16[48,2304]{1,0:T(8,128)(2,1)S(1)}, u32[]{:S(2)}, u32[]{:S(2)}) %collective-permute-start.19) | collective-permute-done | bytes 221216 | tf_op jit(solution)/shard_map/ppermute | solution.py:32
  101.6 4.8 %collective-permute-done.25.refs_4_ = bf16[48,2304]{1,0:T(8,128)(2,1)S(1)} collective-permute-done((bf16[48,2304]{1,0:T(8,128)(2,1)S(1)}, bf16[48,2304]{1,0:T(8,128)(2,1)S(1)}, u32[]{:S(2)}, u32[]{:S(2)}) %collective-permute-start.25) | collective-permute-done | bytes 221216 | tf_op jit(solution)/shard_map/ppermute | solution.py:32
  110.9 5.4 %collective-permute-done.27.refs_1_ = bf16[96,1024]{1,0:T(8,128)(2,1)S(1)} collective-permute-done((bf16[96,1024]{1,0:T(8,128)(2,1)S(1)}, bf16[96,1024]{1,0:T(8,128)(2,1)S(1)}, u32[]{:S(2)}, u32[]{:S(2)}) %collective-permute-start.27) | collective-permute-done | bytes 196640 | tf_op jit(solution)/shard_map/ppermute | solution.py:36
  121.3 7.4 %collective-permute-done.29 = bf16[48,2304]{1,0:T(8,128)(2,1)} collective-permute-done((bf16[48,2304]{1,0:T(8,128)(2,1)}, bf16[48,2304]{1,0:T(8,128)(2,1)}, u32[]{:S(2)}, u32[]{:S(2)}) %collective-permute-start.29) | collective-permute-done | bytes 221216 | tf_op jit(solution)/shard_map/ppermute | solution.py:32
  135.7 5.2 %collective-permute-start.34 = (bf16[48,2304]{1,0:T(8,128)(2,1)S(1)}, bf16[48,2304]{1,0:T(8,128)(2,1)S(1)}, u32[]{:S(2)}, u32[]{:S(2)}) collective-permute-start(bf16[48,2304]{1,0:T(8,128)(2,1)S(1)} %fusion.1), channel_id=1, source_target_pairs={{0,4},{1,5},{2,6},{3,7},{4,0},{5,1},{6,2},{7,3},{8,12},{9,13},{10,... | collective-permute-start | bytes 663560 | tf_op jit(solution)/shard_map/ppermute | solution.py:32
  142.7 3.2 %collective-permute-start.35 = (bf16[48,2304]{1,0:T(8,128)(2,1)S(1)}, bf16[48,2304]{1,0:T(8,128)(2,1)S(1)}, u32[]{:S(2)}, u32[]{:S(2)}) collective-permute-start(bf16[48,2304]{1,0:T(8,128)(2,1)S(1)} %fusion), channel_id=1, source_target_pairs={{0,2},{1,3},{2,0},{3,1},{4,6},{5,7},{6,4},{7,5},{8,10},{9,11},{10,... | collective-permute-start | bytes 663560 | tf_op jit(solution)/shard_map/ppermute | solution.py:32
  147.3 5.3 %collective-permute-done.34.refs_1_ = bf16[48,2304]{1,0:T(8,128)(2,1)S(1)} collective-permute-done((bf16[48,2304]{1,0:T(8,128)(2,1)S(1)}, bf16[48,2304]{1,0:T(8,128)(2,1)S(1)}, u32[]{:S(2)}, u32[]{:S(2)}) %collective-permute-start.34) | collective-permute-done | bytes 221216 | tf_op jit(solution)/shard_map/ppermute | solution.py:32
  160.1 3.2 %collective-permute-done.36.refs_1_.refs_4_ = bf16[48,2304]{1,0:T(8,128)(2,1)S(1)} collective-permute-done((bf16[48,2304]{1,0:T(8,128)(2,1)S(1)}, bf16[48,2304]{1,0:T(8,128)(2,1)S(1)}, u32[]{:S(2)}, u32[]{:S(2)}) %collective-permute-start.36) | collective-permute-done | bytes 221216 | tf_op jit(solution)/shard_map/ppermute | solution.py:32
  170.5 7.2 %collective-permute-done.39._.refs_3_.refs_6_ = bf16[48,2304]{1,0:T(8,128)(2,1)S(1)} collective-permute-done((bf16[48,2304]{1,0:T(8,128)(2,1)S(1)}, bf16[48,2304]{1,0:T(8,128)(2,1)S(1)}, u32[]{:S(2)}, u32[]{:S(2)}) %collective-permute-start.39) | collective-permute-done | bytes 221216 | tf_op jit(solution)/shard_map/ppermute | solution.py:32
  188.8 5.5 %shard_map.121 = (f32[18432,128]{1,0:T(8,128)}, f32[8,128]{1,0:T(8,128)S(1)}) custom-call(bf16[192,1024]{1,0:T(8,128)(2,1)S(1)} %get-tuple-element.93.c0, bf16[192,1024]{1,0:T(8,128)(2,1)S(1)} %get-tuple-element.94.c1, bf16[48,2304]{1,0:T(8,128)(2,1)S(1)} %get-tuple-element.96.refs_1_.refs_0_, bf16[48,2304]{1,0:T(8,128)(2,1)S(1)} %collective-permute-done.37.refs_2_.refs_1_, ...), custom_call_target="tpu_custom_call" | custom-call | flops 20000000000 | bytes 1000 | tf_op jit(solution)/shard_map/pallas_call | solution.py:275
  (123 shorter events, 92.7 us)
Async XLA Ops:
  0.6 15.3 %collective-permute-start = (bf16[48,2304]{1,0:T(8,128)(2,1)}, bf16[48,2304]{1,0:T(8,128)(2,1)S(1)}, u32[]{:S(2)}, u32[]{:S(2)}) collective-permute-start(bf16[48,2304]{1,0:T(8,128)(2,1)} %bitcast.48), channel_id=1, source_target_pairs={{0,2},{1,3},{2,0},{3,1},{4,6},{5,7},{6,4},{7,5},{8,10},{9,11},{10,... | collective-permute-start | bytes 663560 | tf_op jit(solution)/shard_map/ppermute | solution.py:32
  3.7 12.2 %collective-permute-start.1 = (bf16[48,2304]{1,0:T(8,128)(2,1)}, bf16[48,2304]{1,0:T(8,128)(2,1)S(1)}, u32[]{:S(2)}, u32[]{:S(2)}) collective-permute-start(bf16[48,2304]{1,0:T(8,128)(2,1)} %bitcast.49), channel_id=1, source_target_pairs={{0,1},{1,0},{2,3},{3,2},{4,5},{5,4},{6,7},{7,6},{8,9},{9,8},{10,11... | collective-permute-start | bytes 663560 | tf_op jit(solution)/shard_map/ppermute | solution.py:32
  5.2 12.3 %collective-permute-start.4 = (bf16[48,2304]{1,0:T(8,128)(2,1)}, bf16[48,2304]{1,0:T(8,128)(2,1)S(1)}, u32[]{:S(2)}, u32[]{:S(2)}) collective-permute-start(bf16[48,2304]{1,0:T(8,128)(2,1)} %bitcast.50), channel_id=1, source_target_pairs={{0,6},{1,7},{2,4},{3,5},{4,2},{5,3},{6,0},{7,1},{8,14},{9,15},{10,... | collective-permute-start | bytes 663560 | tf_op jit(solution)/shard_map/ppermute | solution.py:32
  7.7 19.4 %collective-permute-start.3 = (bf16[48,2304]{1,0:T(8,128)(2,1)}, bf16[48,2304]{1,0:T(8,128)(2,1)S(1)}, u32[]{:S(2)}, u32[]{:S(2)}) collective-permute-start(bf16[48,2304]{1,0:T(8,128)(2,1)} %bitcast.51), channel_id=1, source_target_pairs={{0,4},{1,5},{2,6},{3,7},{4,0},{5,1},{6,2},{7,3},{8,12},{9,13},{10,... | collective-permute-start | bytes 663560 | tf_op jit(solution)/shard_map/ppermute | solution.py:32
  15.9 11.7 %collective-permute-start.2 = (bf16[48,2304]{1,0:T(8,128)(2,1)S(1)}, bf16[48,2304]{1,0:T(8,128)(2,1)S(1)}, u32[]{:S(2)}, u32[]{:S(2)}) collective-permute-start(bf16[48,2304]{1,0:T(8,128)(2,1)S(1)} %collective-permute-done.refs_0_), channel_id=1, source_target_pairs={{0,1},{1,0},{2,3},{3,2},{4,5},{5,4},{6,7},{7,6},{8,9},{9,8},{10,11... | collective-permute-start | bytes 663560 | tf_op jit(solution)/shard_map/ppermute | solution.py:32
  17.5 10.1 %collective-permute-start.5 = (bf16[48,2304]{1,0:T(8,128)(2,1)S(1)}, bf16[48,2304]{1,0:T(8,128)(2,1)S(1)}, u32[]{:S(2)}, u32[]{:S(2)}) collective-permute-start(bf16[48,2304]{1,0:T(8,128)(2,1)S(1)} %collective-permute-done.4.refs_2_), channel_id=1, source_target_pairs={{0,1},{1,0},{2,3},{3,2},{4,5},{5,4},{6,7},{7,6},{8,9},{9,8},{10,11... | collective-permute-start | bytes 663560 | tf_op jit(solution)/shard_map/ppermute | solution.py:32
  50.4 16.4 %collective-permute-start.13 = (bf16[48,2304]{1,0:T(8,128)(2,1)S(1)}, bf16[48,2304]{1,0:T(8,128)(2,1)S(1)}, u32[]{:S(2)}, u32[]{:S(2)}) collective-permute-start(bf16[48,2304]{1,0:T(8,128)(2,1)S(1)} %fusion.6), channel_id=1, source_target_pairs={{0,6},{1,7},{2,4},{3,5},{4,2},{5,3},{6,0},{7,1},{8,14},{9,15},{10,... | collective-permute-start | bytes 663560 | tf_op jit(solution)/shard_map/ppermute | solution.py:32
  56.9 15.9 %collective-permute-start.14 = (bf16[48,2304]{1,0:T(8,128)(2,1)S(1)}, bf16[48,2304]{1,0:T(8,128)(2,1)S(1)}, u32[]{:S(2)}, u32[]{:S(2)}) collective-permute-start(bf16[48,2304]{1,0:T(8,128)(2,1)S(1)} %fusion.5), channel_id=1, source_target_pairs={{0,4},{1,5},{2,6},{3,7},{4,0},{5,1},{6,2},{7,3},{8,12},{9,13},{10,... | collective-permute-start | bytes 663560 | tf_op jit(solution)/shard_map/ppermute | solution.py:32
  63.2 11.9 %collective-permute-start.15 = (bf16[48,2304]{1,0:T(8,128)(2,1)S(1)}, bf16[48,2304]{1,0:T(8,128)(2,1)S(1)}, u32[]{:S(2)}, u32[]{:S(2)}) collective-permute-start(bf16[48,2304]{1,0:T(8,128)(2,1)S(1)} %fusion.4), channel_id=1, source_target_pairs={{0,2},{1,3},{2,0},{3,1},{4,6},{5,7},{6,4},{7,5},{8,10},{9,11},{10,... | collective-permute-start | bytes 663560 | tf_op jit(solution)/shard_map/ppermute | solution.py:32
  75.1 8.4 %collective-permute-start.16 = (bf16[48,2304]{1,0:T(8,128)(2,1)S(1)}, bf16[48,2304]{1,0:T(8,128)(2,1)S(1)}, u32[]{:S(2)}, u32[]{:S(2)}) collective-permute-start(bf16[48,2304]{1,0:T(8,128)(2,1)S(1)} %add_convert_fusion.refs_1_), channel_id=1, source_target_pairs={{0,2},{1,3},{2,0},{3,1},{4,6},{5,7},{6,4},{7,5},{8,10},{9,11},{10,... | collective-permute-start | bytes 663560 | tf_op jit(solution)/shard_map/ppermute | solution.py:32
  75.2 8.3 %collective-permute-start.17 = (bf16[48,2304]{1,0:T(8,128)(2,1)S(1)}, bf16[48,2304]{1,0:T(8,128)(2,1)S(1)}, u32[]{:S(2)}, u32[]{:S(2)}) collective-permute-start(bf16[48,2304]{1,0:T(8,128)(2,1)S(1)} %add_convert_fusion.refs_1_), channel_id=1, source_target_pairs={{0,1},{1,0},{2,3},{3,2},{4,5},{5,4},{6,7},{7,6},{8,9},{9,8},{10,11... | collective-permute-start | bytes 663560 | tf_op jit(solution)/shard_map/ppermute | solution.py:32
  76.9 11.4 %collective-permute-start.20 = (bf16[48,2304]{1,0:T(8,128)(2,1)S(1)}, bf16[48,2304]{1,0:T(8,128)(2,1)S(1)}, u32[]{:S(2)}, u32[]{:S(2)}) collective-permute-start(bf16[48,2304]{1,0:T(8,128)(2,1)S(1)} %add_convert_fusion.refs_1_), channel_id=1, source_target_pairs={{0,6},{1,7},{2,4},{3,5},{4,2},{5,3},{6,0},{7,1},{8,14},{9,15},{10,... | collective-permute-start | bytes 663560 | tf_op jit(solution)/shard_map/ppermute | solution.py:32
  79.4 17.7 %collective-permute-start.19 = (bf16[48,2304]{1,0:T(8,128)(2,1)S(1)}, bf16[48,2304]{1,0:T(8,128)(2,1)S(1)}, u32[]{:S(2)}, u32[]{:S(2)}) collective-permute-start(bf16[48,2304]{1,0:T(8,128)(2,1)S(1)} %add_convert_fusion.refs_1_), channel_id=1, source_target_pairs={{0,4},{1,5},{2,6},{3,7},{4,0},{5,1},{6,2},{7,3},{8,12},{9,13},{10,... | collective-permute-start | bytes 663560 | tf_op jit(solution)/shard_map/ppermute | solution.py:32
  83.5 13.6 %collective-permute-start.18 = (bf16[48,2304]{1,0:T(8,128)(2,1)S(1)}, bf16[48,2304]{1,0:T(8,128)(2,1)S(1)}, u32[]{:S(2)}, u32[]{:S(2)}) collective-permute-start(bf16[48,2304]{1,0:T(8,128)(2,1)S(1)} %collective-permute-done.16.refs_1_), channel_id=1, source_target_pairs={{0,1},{1,0},{2,3},{3,2},{4,5},{5,4},{6,7},{7,6},{8,9},{9,8},{10,11... | collective-permute-start | bytes 663560 | tf_op jit(solution)/shard_map/ppermute | solution.py:32
  88.2 8.8 %collective-permute-start.21 = (bf16[48,2304]{1,0:T(8,128)(2,1)S(1)}, bf16[48,2304]{1,0:T(8,128)(2,1)S(1)}, u32[]{:S(2)}, u32[]{:S(2)}) collective-permute-start(bf16[48,2304]{1,0:T(8,128)(2,1)S(1)} %collective-permute-done.20._.refs_3_), channel_id=1, source_target_pairs={{0,1},{1,0},{2,3},{3,2},{4,5},{5,4},{6,7},{7,6},{8,9},{9,8},{10,11... | collective-permute-start | bytes 663560 | tf_op jit(solution)/shard_map/ppermute | solution.py:32
  130.0 15.8 %collective-permute-start.33 = (bf16[48,2304]{1,0:T(8,128)(2,1)S(1)}, bf16[48,2304]{1,0:T(8,128)(2,1)S(1)}, u32[]{:S(2)}, u32[]{:S(2)}) collective-permute-start(bf16[48,2304]{1,0:T(8,128)(2,1)S(1)} %fusion.2), channel_id=1, source_target_pairs={{0,6},{1,7},{2,4},{3,5},{4,2},{5,3},{6,0},{7,1},{8,14},{9,15},{10,... | collective-permute-start | bytes 663560 | tf_op jit(solution)/shard_map/ppermute | solution.py:32
  135.7 16.8 %collective-permute-start.34 = (bf16[48,2304]{1,0:T(8,128)(2,1)S(1)}, bf16[48,2304]{1,0:T(8,128)(2,1)S(1)}, u32[]{:S(2)}, u32[]{:S(2)}) collective-permute-start(bf16[48,2304]{1,0:T(8,128)(2,1)S(1)} %fusion.1), channel_id=1, source_target_pairs={{0,4},{1,5},{2,6},{3,7},{4,0},{5,1},{6,2},{7,3},{8,12},{9,13},{10,... | collective-permute-start | bytes 663560 | tf_op jit(solution)/shard_map/ppermute | solution.py:32
  142.7 11.8 %collective-permute-start.35 = (bf16[48,2304]{1,0:T(8,128)(2,1)S(1)}, bf16[48,2304]{1,0:T(8,128)(2,1)S(1)}, u32[]{:S(2)}, u32[]{:S(2)}) collective-permute-start(bf16[48,2304]{1,0:T(8,128)(2,1)S(1)} %fusion), channel_id=1, source_target_pairs={{0,2},{1,3},{2,0},{3,1},{4,6},{5,7},{6,4},{7,5},{8,10},{9,11},{10,... | collective-permute-start | bytes 663560 | tf_op jit(solution)/shard_map/ppermute | solution.py:32
  156.6 12.2 %collective-permute-start.40 = (bf16[48,2304]{1,0:T(8,128)(2,1)S(1)}, bf16[48,2304]{1,0:T(8,128)(2,1)S(1)}, u32[]{:S(2)}, u32[]{:S(2)}) collective-permute-start(bf16[48,2304]{1,0:T(8,128)(2,1)S(1)} %get-tuple-element.96.refs_1_.refs_0_), channel_id=1, source_target_pairs={{0,6},{1,7},{2,4},{3,5},{4,2},{5,3},{6,0},{7,1},{8,14},{9,15},{10,... | collective-permute-start | bytes 663560 | tf_op jit(solution)/shard_map/ppermute | solution.py:32
  159.5 18.1 %collective-permute-start.39 = (bf16[48,2304]{1,0:T(8,128)(2,1)S(1)}, bf16[48,2304]{1,0:T(8,128)(2,1)S(1)}, u32[]{:S(2)}, u32[]{:S(2)}) collective-permute-start(bf16[48,2304]{1,0:T(8,128)(2,1)S(1)} %get-tuple-element.96.refs_1_.refs_0_), channel_id=1, source_target_pairs={{0,4},{1,5},{2,6},{3,7},{4,0},{5,1},{6,2},{7,3},{8,12},{9,13},{10,... | collective-permute-start | bytes 663560 | tf_op jit(solution)/shard_map/ppermute | solution.py:32
  163.3 17.0 %collective-permute-start.38 = (bf16[48,2304]{1,0:T(8,128)(2,1)S(1)}, bf16[48,2304]{1,0:T(8,128)(2,1)S(1)}, u32[]{:S(2)}, u32[]{:S(2)}) collective-permute-start(bf16[48,2304]{1,0:T(8,128)(2,1)S(1)} %collective-permute-done.36.refs_1_.refs_4_), channel_id=1, source_target_pairs={{0,1},{1,0},{2,3},{3,2},{4,5},{5,4},{6,7},{7,6},{8,9},{9,8},{10,11... | collective-permute-start | bytes 663560 | tf_op jit(solution)/shard_map/ppermute | solution.py:32
  168.8 11.5 %collective-permute-start.41 = (bf16[48,2304]{1,0:T(8,128)(2,1)S(1)}, bf16[48,2304]{1,0:T(8,128)(2,1)S(1)}, u32[]{:S(2)}, u32[]{:S(2)}) collective-permute-start(bf16[48,2304]{1,0:T(8,128)(2,1)S(1)} %collective-permute-done.40.refs_3_.refs_2_), channel_id=1, source_target_pairs={{0,1},{1,0},{2,3},{3,2},{4,5},{5,4},{6,7},{7,6},{8,9},{9,8},{10,11... | collective-permute-start | bytes 663560 | tf_op jit(solution)/shard_map/ppermute | solution.py:32
  185.9 8.4 %collective-permute-start.45 = (bf16[96,1024]{1,0:T(8,128)(2,1)S(1)}, bf16[96,1024]{1,0:T(8,128)(2,1)S(1)}, u32[]{:S(2)}, u32[]{:S(2)}) collective-permute-start(bf16[96,1024]{1,0:T(8,128)(2,1)S(1)} %add_convert_fusion.2.refs_1_), channel_id=1, source_target_pairs={{0,16},{16,0},{1,17},{17,1},{2,18},{18,2},{3,19},{19,3},{4,20},{20... | collective-permute-start | bytes 589832 | tf_op jit(solution)/shard_map/ppermute | solution.py:36
  187.5 9.8 %collective-permute-start.47 = (bf16[96,1024]{1,0:T(8,128)(2,1)S(1)}, bf16[96,1024]{1,0:T(8,128)(2,1)S(1)}, u32[]{:S(2)}, u32[]{:S(2)}) collective-permute-start(bf16[96,1024]{1,0:T(8,128)(2,1)S(1)} %add_convert_fusion.1.refs_8_.refs_1_), channel_id=1, source_target_pairs={{0,16},{16,0},{1,17},{17,1},{2,18},{18,2},{3,19},{19,3},{4,20},{20... | collective-permute-start | bytes 589832 | tf_op jit(solution)/shard_map/ppermute | solution.py:36
  (30 other events, 214.5 us)

commit v3 on v2

--- a/solution.py
+++ b/solution.py
@@ -36,15 +36,22 @@
     return lax.ppermute(x, axis, SWAP2)
 
 
-def gather(x, first=(), mid=(), weight=None):
+def gather(x, first=(), mid=()):
     z1, y0, z3, z2 = swap(x, 2), swap(x, 1), swap(x, 6), swap(x, 4)
     y1 = swap(after(z1, y0), 1)
     y3 = swap(after(z3, *first), 1)
-    if weight is not None:
-        weight = load_after(weight, z3)
-        mid = (weight,)
     y2 = swap(after(z2, *mid), 1)
-    return (after(x, y1, z2), y0, z3, y3), (z1, y1, z2, y2), weight
+    return (after(x, y1, z2), y0, z3, y3), (z1, y1, z2, y2)
+
+
+def gather_with(x, weight, work):
+    z1, y0, z3, z2 = swap(x, 2), swap(x, 1), swap(x, 6), swap(x, 4)
+    y1 = swap(after(z1, y0), 1)
+    y3 = swap(z3, 1)
+    weight = load_after(weight, z3)
+    done = work((after(x, y1), y0, z3, y3), weight)
+    y2 = swap(after(z2, done[0]), 1)
+    return done, weight, (z1, y1, z2, y2), (x, y0, z3, y3)
 
 
 def call(kernel, grid, in_specs, out_specs, out_shape, scratch=(), mib=24):
@@ -358,7 +365,7 @@
     gate_l = load(gate_l)
     up_l = load(up_l, gate_l)
     down_l = load(down_l, up_l)
-    xa, xb, _ = gather(inputs[0], (up_l,), (down_l,))
+    xa, xb = gather(inputs[0], (up_l,), (down_l,))
     gl = after(gate_l, down_l)
     ga = gate_up(xa, gl, up_l)
     gb = gate_up((after(xb[0], ga),) + xb[1:], gate_l, up_l)
@@ -366,8 +373,8 @@
     pb = down(gb, pair(gb, "tok"), after(down_l, pa[0]))
     acts = scatter(pa, pb).astype(BF16)
 
-    aa, ab, enc_2 = gather(acts, weight=enc_l)
-    qa = chip_sum(*encode(tok, aa, enc_2))
+    ea, enc_2, ab, _ = gather_with(acts, enc_l, lambda b, w: encode(tok, b, w))
+    qa = chip_sum(*ea)
     ha = to_codes(qa, bias)
     mine, away = encode(tok, (after(ab[0], qa),) + ab[1:], enc_2)
     halves = [ha, to_codes(chip_sum(after(mine, ha), away), bias)]
@@ -375,13 +382,14 @@
     ca, cb, *r = decode(tok, *joined, dec_l)
     err = scatter(r[:3], r[3:]) + dec_bias[0] - acts.astype(F32)
 
-    ea, eb, _ = gather(err.astype(BF16))
-    dec_3 = load_after(dec_l, eb[2])
-    mine, away = latent(tok, ea, dec_3)
-    la = chip_sum(after(mine, eb[3]), away)
-    lb = chip_sum(*latent(tok, (after(eb[0], la),) + eb[1:], dec_3))
+    err_b = err.astype(BF16)
+    lat_a, dec_3, eb, ea = gather_with(err_b, dec_l, lambda b, w: latent(tok, b, w))
+    la = chip_sum(*lat_a)
+    sa = add(la, pair(la, "mp"))
+    mine, away = latent(tok, (after(eb[0], la),) + eb[1:], dec_3)
+    lb = chip_sum(after(mine, sa), away)
     dec_grad, t = decoder_grad((ca, cb), ea + eb, lb)
-    la, lb = [add(l, pair(l, "mp"), first=(t,)) for l in (la, lb)]
+    la, lb = sa, add(lb, pair(lb, "mp"), first=(t,))
     who = jnp.concatenate([me.reshape(1), tok])
     lat = ordered(who, la, pair(la, "tok"), lb, pair(lb, "tok"))
     return (err[None], dec_grad, lat)

time: 201 us -> 195 us (0.970)
  waiting for transfers between devices: 81.8 us -> 71.7 us
  starting transfers between devices: 64.8 us -> 69.2 us
    ppermute x35, waiting for transfers between devices: 67.9 us -> 61.1 us  [swap(): return lax.ppermute(x, 'lat', [(i, i ^ k) for i in range(8)])]
    ppermute x35, starting transfers between devices: 58.1 us -> 61.4 us  [swap(): return lax.ppermute(x, 'lat', [(i, i ^ k) for i in range(8)])]
    ppermute x14, waiting for transfers between devices: 13.9 us -> 10.6 us  [pair(): return lax.ppermute(x, axis, SWAP2)]
  transfers between devices with their start and end apart: 49 -> 49, of which waited for: 30 -> 29; matrix products, arithmetic and copies ran while one was open for 1% -> 1% of each run, Pallas kernels for 21% -> 24%
where the time goes in v3:
time: 195 us
  waiting for transfers between devices  71.7 us (37%)
  starting transfers between devices  69.2 us (35%)
  Pallas kernels  50.6 us (26%)
  other arithmetic  2.55 us (1%)
    ppermute x35, starting transfers between devices, swap(): return lax.ppermute(x, 'lat', [(i, i ^ k) for i in range(8)])  61.4 us
    ppermute x35, waiting for transfers between devices, swap(): return lax.ppermute(x, 'lat', [(i, i ^ k) for i in range(8)])  61.1 us
    pallas_call x15, Pallas kernels, vmem_call(): pl.pallas_call(lambda *refs: kernel(*refs[k:]), in_specs=[pl.BlockSpec(me...  26.5 us
    pallas_call x3, Pallas kernels, load(): pl.pallas_call(load_kernel, in_specs=[pl.BlockSpec(memory_space=pltpu.HBM...  12.1 us
    ppermute x14, waiting for transfers between devices, pair(): return lax.ppermute(x, axis, SWAP2)  10.6 us
    ppermute x14, starting transfers between devices, pair(): return lax.ppermute(x, axis, SWAP2)  7.82 us
    pallas_call x1, Pallas kernels, decoder_grad(): call(grad_kernel, (n // step,), [cspec, cspec] + [whole(blocks[0])] * 8 +...  5.46 us
    pallas_call x2, Pallas kernels, load_after(): pl.pallas_call(kernel, in_specs=[pl.BlockSpec(memory_space=pl.ANY), pl.Bl...  4.84 us
  transfers between devices with their start and end apart: 49, of which 29 were waited for; matrix products, arithmetic and copies ran while one was open for 1% of the time, Pallas kernels for 24%

profile of v3, /device:TPU:0, one launch (start us, length us, event | category | flops | bytes accessed | tf_op | source)
XLA Modules:
  0.0 195.1 jit_solution(4461044919303391718)
XLA Ops:
  0.6 3.1 %collective-permute-start = (bf16[48,2304]{1,0:T(8,128)(2,1)}, bf16[48,2304]{1,0:T(8,128)(2,1)S(1)}, u32[]{:S(2)}, u32[]{:S(2)}) collective-permute-start(bf16[48,2304]{1,0:T(8,128)(2,1)} %bitcast.48), channel_id=1, source_target_pairs={{0,2},{1,3},{2,0},{3,1},{4,6},{5,7},{6,4},{7,5},{8,10},{9,11},{10,... | collective-permute-start | bytes 663560 | tf_op jit(solution)/shard_map/ppermute | solution.py:32
  7.8 4.0 %shard_map.103.refs_4_ = bf16[2304,2304]{1,0:T(8,128)(2,1)S(1)} custom-call(bf16[2304,2304]{1,0:T(8,128)(2,1)} %bitcast.55), custom_call_target="tpu_custom_call" | custom-call | flops 1000 | bytes 1000 | tf_op jit(solution)/shard_map/pallas_call | solution.py:108
  11.9 4.0 %shard_map.104.refs_5_ = bf16[2304,2304]{1,0:T(8,128)(2,1)S(1)} custom-call(bf16[2304,2304]{1,0:T(8,128)(2,1)} %bitcast.56), custom_call_target="tpu_custom_call" | custom-call | flops 1000 | bytes 1000 | tf_op jit(solution)/shard_map/pallas_call | solution.py:108
  19.1 4.1 %shard_map.105.refs_2_ = bf16[2304,2304]{1,0:T(8,128)(2,1)S(1)} custom-call(bf16[2304,2304]{1,0:T(8,128)(2,1)} %bitcast.57), custom_call_target="tpu_custom_call" | custom-call | flops 1000 | bytes 1000 | tf_op jit(solution)/shard_map/pallas_call | solution.py:108
  23.1 4.0 %collective-permute-done.3.refs_2_ = bf16[48,2304]{1,0:T(8,128)(2,1)S(1)} collective-permute-done((bf16[48,2304]{1,0:T(8,128)(2,1)}, bf16[48,2304]{1,0:T(8,128)(2,1)S(1)}, u32[]{:S(2)}, u32[]{:S(2)}) %collective-permute-start.3) | collective-permute-done | bytes 221216 | tf_op jit(solution)/shard_map/ppermute | solution.py:32
  27.7 4.7 %shard_map.106.refs_0_ = bf16[2,192,2304]{2,1,0:T(8,128)(2,1)S(1)} custom-call(bf16[48,2304]{1,0:T(8,128)(2,1)S(1)} %bitcast.52, bf16[48,2304]{1,0:T(8,128)(2,1)S(1)} %collective-permute-done.1.refs_1_, bf16[48,2304]{1,0:T(8,128)(2,1)S(1)} %collective-permute-done.4.refs_2_, bf16[48,2304]{1,0:T(8,128)(2,1)S(1)} %collective-permute-done.5.refs_3_, ...), custom_call_target="tpu_custom_call" | custom-call | flops 1000 | bytes 1000 | tf_op jit(solution)/shard_map/pallas_call | solution.py:88
  33.1 4.7 %shard_map.107.refs_0_ = bf16[2,192,2304]{2,1,0:T(8,128)(2,1)S(1)} custom-call(bf16[48,2304]{1,0:T(8,128)(2,1)S(1)} %collective-permute-done.refs_0_, bf16[48,2304]{1,0:T(8,128)(2,1)S(1)} %collective-permute-done.2.refs_1_, bf16[48,2304]{1,0:T(8,128)(2,1)S(1)} %collective-permute-done.3.refs_2_, bf16[48,2304]{1,0:T(8,128)(2,1)S(1)} %collective-permute-done.7.refs_3_, ...), custom_call_target="tpu_custom_call" | custom-call | flops 1000 | bytes 1000 | tf_op jit(solution)/shard_map/pallas_call | solution.py:88
  38.0 3.6 %shard_map.108 = (f32[2,48,2304]{2,1,0:T(8,128)S(1)}, bf16[48,2304]{1,0:T(8,128)(2,1)S(1)}, bf16[48,2304]{1,0:T(8,128)(2,1)S(1)}) custom-call(bf16[2,192,2304]{2,1,0:T(8,128)(2,1)S(1)} %shard_map.106.refs_0_, bf16[2,192,2304]{2,1,0:T(8,128)(2,1)S(1)} %collective-permute-done.6.refs_1_, bf16[2304,2304]{1,0:T(8,128)(2,1)S(1)} %shard_map.105.refs_2_), custom_call_target="tpu_custom_call" | custom-call | flops 1000 | bytes 1000 | tf_op jit(solution)/shard_map/pallas_call | solution.py:88
  43.0 3.6 %shard_map.109 = (f32[2,48,2304]{2,1,0:T(8,128)S(1)}, bf16[48,2304]{1,0:T(8,128)(2,1)S(1)}, bf16[48,2304]{1,0:T(8,128)(2,1)S(1)}) custom-call(bf16[2,192,2304]{2,1,0:T(8,128)(2,1)S(1)} %shard_map.107.refs_0_, bf16[2,192,2304]{2,1,0:T(8,128)(2,1)S(1)} %collective-permute-done.8.refs_1_, bf16[2304,2304]{1,0:T(8,128)(2,1)S(1)} %shard_map.105.refs_2_), custom_call_target="tpu_custom_call" | custom-call | flops 1000 | bytes 1000 | tf_op jit(solution)/shard_map/pallas_call | solution.py:88
  53.1 3.4 %collective-permute-done.10 = bf16[48,2304]{1,0:T(8,128)(2,1)S(1)} collective-permute-done((bf16[48,2304]{1,0:T(8,128)(2,1)S(1)}, bf16[48,2304]{1,0:T(8,128)(2,1)S(1)}, u32[]{:S(2)}, u32[]{:S(2)}) %collective-permute-start.10) | collective-permute-done | bytes 221216 | tf_op jit(solution)/shard_map/ppermute | solution.py:32
  56.9 4.8 %collective-permute-start.14 = (bf16[48,2304]{1,0:T(8,128)(2,1)S(1)}, bf16[48,2304]{1,0:T(8,128)(2,1)S(1)}, u32[]{:S(2)}, u32[]{:S(2)}) collective-permute-start(bf16[48,2304]{1,0:T(8,128)(2,1)S(1)} %fusion.5), channel_id=1, source_target_pairs={{0,4},{1,5},{2,6},{3,7},{4,0},{5,1},{6,2},{7,3},{8,12},{9,13},{10,... | collective-permute-start | bytes 663560 | tf_op jit(solution)/shard_map/ppermute | solution.py:32
  63.2 3.6 %collective-permute-start.15 = (bf16[48,2304]{1,0:T(8,128)(2,1)S(1)}, bf16[48,2304]{1,0:T(8,128)(2,1)S(1)}, u32[]{:S(2)}, u32[]{:S(2)}) collective-permute-start(bf16[48,2304]{1,0:T(8,128)(2,1)S(1)} %fusion.4), channel_id=1, source_target_pairs={{0,2},{1,3},{2,0},{3,1},{4,6},{5,7},{6,4},{7,5},{8,10},{9,11},{10,... | collective-permute-start | bytes 663560 | tf_op jit(solution)/shard_map/ppermute | solution.py:32
  68.6 4.2 %collective-permute-done.14.refs_1_ = bf16[48,2304]{1,0:T(8,128)(2,1)S(1)} collective-permute-done((bf16[48,2304]{1,0:T(8,128)(2,1)S(1)}, bf16[48,2304]{1,0:T(8,128)(2,1)S(1)}, u32[]{:S(2)}, u32[]{:S(2)}) %collective-permute-start.14) | collective-permute-done | bytes 221216 | tf_op jit(solution)/shard_map/ppermute | solution.py:32
  79.4 4.1 %collective-permute-done.16.refs_1_ = bf16[48,2304]{1,0:T(8,128)(2,1)S(1)} collective-permute-done((bf16[48,2304]{1,0:T(8,128)(2,1)S(1)}, bf16[48,2304]{1,0:T(8,128)(2,1)S(1)}, u32[]{:S(2)}, u32[]{:S(2)}) %collective-permute-start.16) | collective-permute-done | bytes 221216 | tf_op jit(solution)/shard_map/ppermute | solution.py:32
  97.9 4.4 %collective-permute-done.25.refs_4_ = bf16[48,2304]{1,0:T(8,128)(2,1)S(1)} collective-permute-done((bf16[48,2304]{1,0:T(8,128)(2,1)S(1)}, bf16[48,2304]{1,0:T(8,128)(2,1)S(1)}, u32[]{:S(2)}, u32[]{:S(2)}) %collective-permute-start.25) | collective-permute-done | bytes 221216 | tf_op jit(solution)/shard_map/ppermute | solution.py:32
  106.8 5.4 %collective-permute-done.27.refs_1_ = bf16[96,1024]{1,0:T(8,128)(2,1)S(1)} collective-permute-done((bf16[96,1024]{1,0:T(8,128)(2,1)S(1)}, bf16[96,1024]{1,0:T(8,128)(2,1)S(1)}, u32[]{:S(2)}, u32[]{:S(2)}) %collective-permute-start.27) | collective-permute-done | bytes 196640 | tf_op jit(solution)/shard_map/ppermute | solution.py:36
  113.8 3.0 %shard_map.116 = (bf16[192,1024]{1,0:T(8,128)(2,1)S(1)}, bf16[192,1024]{1,0:T(8,128)(2,1)S(1)}, f32[2,48,2304]{2,1,0:T(8,128)S(1)}, bf16[48,2304]{1,0:T(8,128)(2...) custom-call(s32[1]{0:T(128)} %bitcast.refs_0_, ...), custom_call_target="tpu_custom_call" | custom-call | flops 1000 | bytes 1000 | tf_op jit(solution)/shard_map/pallas_call | solution.py:88
  118.6 6.0 %collective-permute-done.29 = bf16[48,2304]{1,0:T(8,128)(2,1)} collective-permute-done((bf16[48,2304]{1,0:T(8,128)(2,1)}, bf16[48,2304]{1,0:T(8,128)(2,1)}, u32[]{:S(2)}, u32[]{:S(2)}) %collective-permute-start.29) | collective-permute-done | bytes 221216 | tf_op jit(solution)/shard_map/ppermute | solution.py:32
  127.3 3.7 %collective-permute-start.33 = (bf16[48,2304]{1,0:T(8,128)(2,1)S(1)}, bf16[48,2304]{1,0:T(8,128)(2,1)S(1)}, u32[]{:S(2)}, u32[]{:S(2)}) collective-permute-start(bf16[48,2304]{1,0:T(8,128)(2,1)S(1)} %fusion.2), channel_id=1, source_target_pairs={{0,6},{1,7},{2,4},{3,5},{4,2},{5,3},{6,0},{7,1},{8,14},{9,15},{10,... | collective-permute-start | bytes 663560 | tf_op jit(solution)/shard_map/ppermute | solution.py:32
  143.1 6.8 %collective-permute-done.34.refs_1_ = bf16[48,2304]{1,0:T(8,128)(2,1)S(1)} collective-permute-done((bf16[48,2304]{1,0:T(8,128)(2,1)S(1)}, bf16[48,2304]{1,0:T(8,128)(2,1)S(1)}, u32[]{:S(2)}, u32[]{:S(2)}) %collective-permute-start.34) | collective-permute-done | bytes 221216 | tf_op jit(solution)/shard_map/ppermute | solution.py:32
  154.6 3.5 %collective-permute-done.36.refs_2_.refs_1_ = bf16[48,2304]{1,0:T(8,128)(2,1)S(1)} collective-permute-done((bf16[48,2304]{1,0:T(8,128)(2,1)S(1)}, bf16[48,2304]{1,0:T(8,128)(2,1)S(1)}, u32[]{:S(2)}, u32[]{:S(2)}) %collective-permute-start.36) | collective-permute-done | bytes 221216 | tf_op jit(solution)/shard_map/ppermute | solution.py:32
  161.1 3.6 %collective-permute-start.40 = (bf16[48,2304]{1,0:T(8,128)(2,1)S(1)}, bf16[48,2304]{1,0:T(8,128)(2,1)S(1)}, u32[]{:S(2)}, u32[]{:S(2)}) collective-permute-start(bf16[48,2304]{1,0:T(8,128)(2,1)S(1)} %collective-permute-done.39.refs_1_.refs_4_), channel_id=1, source_target_pairs={{0,1},{1,0},{2,3},{3,2},{4,5},{5,4},{6,7},{7,6},{8,9},{9,8},{10,11... | collective-permute-start | bytes 663560 | tf_op jit(solution)/shard_map/ppermute | solution.py:32
  177.5 3.5 %collective-permute-done.42.refs_4_.refs_7_ = bf16[48,2304]{1,0:T(8,128)(2,1)S(1)} collective-permute-done((bf16[48,2304]{1,0:T(8,128)(2,1)S(1)}, bf16[48,2304]{1,0:T(8,128)(2,1)S(1)}, u32[]{:S(2)}, u32[]{:S(2)}) %collective-permute-start.42) | collective-permute-done | bytes 221216 | tf_op jit(solution)/shard_map/ppermute | solution.py:32
  186.1 5.5 %shard_map.122 = (f32[18432,128]{1,0:T(8,128)}, f32[8,128]{1,0:T(8,128)S(1)}) custom-call(bf16[192,1024]{1,0:T(8,128)(2,1)S(1)} %get-tuple-element.94.c0, bf16[192,1024]{1,0:T(8,128)(2,1)S(1)} %get-tuple-element.95.c1, bf16[48,2304]{1,0:T(8,128)(2,1)S(1)} %get-tuple-element.97.refs_1_.refs_0_, bf16[48,2304]{1,0:T(8,128)(2,1)S(1)} %collective-permute-done.36.refs_2_.refs_1_, ...), custom_call_target="tpu_custom_call" | custom-call | flops 20000000000 | bytes 1000 | tf_op jit(solution)/shard_map/pallas_call | solution.py:282
  (123 shorter events, 92.7 us)
Async XLA Ops:
  0.6 15.3 %collective-permute-start = (bf16[48,2304]{1,0:T(8,128)(2,1)}, bf16[48,2304]{1,0:T(8,128)(2,1)S(1)}, u32[]{:S(2)}, u32[]{:S(2)}) collective-permute-start(bf16[48,2304]{1,0:T(8,128)(2,1)} %bitcast.48), channel_id=1, source_target_pairs={{0,2},{1,3},{2,0},{3,1},{4,6},{5,7},{6,4},{7,5},{8,10},{9,11},{10,... | collective-permute-start | bytes 663560 | tf_op jit(solution)/shard_map/ppermute | solution.py:32
  3.7 12.2 %collective-permute-start.1 = (bf16[48,2304]{1,0:T(8,128)(2,1)}, bf16[48,2304]{1,0:T(8,128)(2,1)S(1)}, u32[]{:S(2)}, u32[]{:S(2)}) collective-permute-start(bf16[48,2304]{1,0:T(8,128)(2,1)} %bitcast.49), channel_id=1, source_target_pairs={{0,1},{1,0},{2,3},{3,2},{4,5},{5,4},{6,7},{7,6},{8,9},{9,8},{10,11... | collective-permute-start | bytes 663560 | tf_op jit(solution)/shard_map/ppermute | solution.py:32
  5.2 12.3 %collective-permute-start.4 = (bf16[48,2304]{1,0:T(8,128)(2,1)}, bf16[48,2304]{1,0:T(8,128)(2,1)S(1)}, u32[]{:S(2)}, u32[]{:S(2)}) collective-permute-start(bf16[48,2304]{1,0:T(8,128)(2,1)} %bitcast.50), channel_id=1, source_target_pairs={{0,6},{1,7},{2,4},{3,5},{4,2},{5,3},{6,0},{7,1},{8,14},{9,15},{10,... | collective-permute-start | bytes 663560 | tf_op jit(solution)/shard_map/ppermute | solution.py:32
  7.7 19.4 %collective-permute-start.3 = (bf16[48,2304]{1,0:T(8,128)(2,1)}, bf16[48,2304]{1,0:T(8,128)(2,1)S(1)}, u32[]{:S(2)}, u32[]{:S(2)}) collective-permute-start(bf16[48,2304]{1,0:T(8,128)(2,1)} %bitcast.51), channel_id=1, source_target_pairs={{0,4},{1,5},{2,6},{3,7},{4,0},{5,1},{6,2},{7,3},{8,12},{9,13},{10,... | collective-permute-start | bytes 663560 | tf_op jit(solution)/shard_map/ppermute | solution.py:32
  15.9 11.7 %collective-permute-start.2 = (bf16[48,2304]{1,0:T(8,128)(2,1)S(1)}, bf16[48,2304]{1,0:T(8,128)(2,1)S(1)}, u32[]{:S(2)}, u32[]{:S(2)}) collective-permute-start(bf16[48,2304]{1,0:T(8,128)(2,1)S(1)} %collective-permute-done.refs_0_), channel_id=1, source_target_pairs={{0,1},{1,0},{2,3},{3,2},{4,5},{5,4},{6,7},{7,6},{8,9},{9,8},{10,11... | collective-permute-start | bytes 663560 | tf_op jit(solution)/shard_map/ppermute | solution.py:32
  17.5 10.1 %collective-permute-start.5 = (bf16[48,2304]{1,0:T(8,128)(2,1)S(1)}, bf16[48,2304]{1,0:T(8,128)(2,1)S(1)}, u32[]{:S(2)}, u32[]{:S(2)}) collective-permute-start(bf16[48,2304]{1,0:T(8,128)(2,1)S(1)} %collective-permute-done.4.refs_2_), channel_id=1, source_target_pairs={{0,1},{1,0},{2,3},{3,2},{4,5},{5,4},{6,7},{7,6},{8,9},{9,8},{10,11... | collective-permute-start | bytes 663560 | tf_op jit(solution)/shard_map/ppermute | solution.py:32
  41.6 7.9 %collective-permute-start.9 = (bf16[48,2304]{1,0:T(8,128)(2,1)S(1)}, bf16[48,2304]{1,0:T(8,128)(2,1)S(1)}, u32[]{:S(2)}, u32[]{:S(2)}) collective-permute-start(bf16[48,2304]{1,0:T(8,128)(2,1)S(1)} %get-tuple-element.69), channel_id=1, source_target_pairs={{0,1},{1,0},{2,3},{3,2},{4,5},{5,4},{6,7},{7,6},{8,9},{9,8},{10,11... | collective-permute-start | bytes 663560 | tf_op jit(solution)/shard_map/ppermute | solution.py:32
  50.4 16.4 %collective-permute-start.13 = (bf16[48,2304]{1,0:T(8,128)(2,1)S(1)}, bf16[48,2304]{1,0:T(8,128)(2,1)S(1)}, u32[]{:S(2)}, u32[]{:S(2)}) collective-permute-start(bf16[48,2304]{1,0:T(8,128)(2,1)S(1)} %fusion.6), channel_id=1, source_target_pairs={{0,6},{1,7},{2,4},{3,5},{4,2},{5,3},{6,0},{7,1},{8,14},{9,15},{10,... | collective-permute-start | bytes 663560 | tf_op jit(solution)/shard_map/ppermute | solution.py:32
  56.9 15.9 %collective-permute-start.14 = (bf16[48,2304]{1,0:T(8,128)(2,1)S(1)}, bf16[48,2304]{1,0:T(8,128)(2,1)S(1)}, u32[]{:S(2)}, u32[]{:S(2)}) collective-permute-start(bf16[48,2304]{1,0:T(8,128)(2,1)S(1)} %fusion.5), channel_id=1, source_target_pairs={{0,4},{1,5},{2,6},{3,7},{4,0},{5,1},{6,2},{7,3},{8,12},{9,13},{10,... | collective-permute-start | bytes 663560 | tf_op jit(solution)/shard_map/ppermute | solution.py:32
  63.2 11.9 %collective-permute-start.15 = (bf16[48,2304]{1,0:T(8,128)(2,1)S(1)}, bf16[48,2304]{1,0:T(8,128)(2,1)S(1)}, u32[]{:S(2)}, u32[]{:S(2)}) collective-permute-start(bf16[48,2304]{1,0:T(8,128)(2,1)S(1)} %fusion.4), channel_id=1, source_target_pairs={{0,2},{1,3},{2,0},{3,1},{4,6},{5,7},{6,4},{7,5},{8,10},{9,11},{10,... | collective-permute-start | bytes 663560 | tf_op jit(solution)/shard_map/ppermute | solution.py:32
  75.1 8.4 %collective-permute-start.16 = (bf16[48,2304]{1,0:T(8,128)(2,1)S(1)}, bf16[48,2304]{1,0:T(8,128)(2,1)S(1)}, u32[]{:S(2)}, u32[]{:S(2)}) collective-permute-start(bf16[48,2304]{1,0:T(8,128)(2,1)S(1)} %add_convert_fusion.refs_1_), channel_id=1, source_target_pairs={{0,2},{1,3},{2,0},{3,1},{4,6},{5,7},{6,4},{7,5},{8,10},{9,11},{10,... | collective-permute-start | bytes 663560 | tf_op jit(solution)/shard_map/ppermute | solution.py:32
  75.2 8.3 %collective-permute-start.17 = (bf16[48,2304]{1,0:T(8,128)(2,1)S(1)}, bf16[48,2304]{1,0:T(8,128)(2,1)S(1)}, u32[]{:S(2)}, u32[]{:S(2)}) collective-permute-start(bf16[48,2304]{1,0:T(8,128)(2,1)S(1)} %add_convert_fusion.refs_1_), channel_id=1, source_target_pairs={{0,1},{1,0},{2,3},{3,2},{4,5},{5,4},{6,7},{7,6},{8,9},{9,8},{10,11... | collective-permute-start | bytes 663560 | tf_op jit(solution)/shard_map/ppermute | solution.py:32
  76.9 9.1 %collective-permute-start.19 = (bf16[48,2304]{1,0:T(8,128)(2,1)S(1)}, bf16[48,2304]{1,0:T(8,128)(2,1)S(1)}, u32[]{:S(2)}, u32[]{:S(2)}) collective-permute-start(bf16[48,2304]{1,0:T(8,128)(2,1)S(1)} %add_convert_fusion.refs_1_), channel_id=1, source_target_pairs={{0,6},{1,7},{2,4},{3,5},{4,2},{5,3},{6,0},{7,1},{8,14},{9,15},{10,... | collective-permute-start | bytes 663560 | tf_op jit(solution)/shard_map/ppermute | solution.py:32
  83.5 9.1 %collective-permute-start.18 = (bf16[48,2304]{1,0:T(8,128)(2,1)S(1)}, bf16[48,2304]{1,0:T(8,128)(2,1)S(1)}, u32[]{:S(2)}, u32[]{:S(2)}) collective-permute-start(bf16[48,2304]{1,0:T(8,128)(2,1)S(1)} %collective-permute-done.16.refs_1_), channel_id=1, source_target_pairs={{0,1},{1,0},{2,3},{3,2},{4,5},{5,4},{6,7},{7,6},{8,9},{9,8},{10,11... | collective-permute-start | bytes 663560 | tf_op jit(solution)/shard_map/ppermute | solution.py:32
  94.7 7.5 %collective-permute-start.25 = (bf16[48,2304]{1,0:T(8,128)(2,1)S(1)}, bf16[48,2304]{1,0:T(8,128)(2,1)S(1)}, u32[]{:S(2)}, u32[]{:S(2)}) collective-permute-start(bf16[48,2304]{1,0:T(8,128)(2,1)S(1)} %collective-permute-done.24.refs_3_), channel_id=1, source_target_pairs={{0,1},{1,0},{2,3},{3,2},{4,5},{5,4},{6,7},{7,6},{8,9},{9,8},{10,11... | collective-permute-start | bytes 663560 | tf_op jit(solution)/shard_map/ppermute | solution.py:32
  116.8 7.8 %collective-permute-start.29 = (bf16[48,2304]{1,0:T(8,128)(2,1)}, bf16[48,2304]{1,0:T(8,128)(2,1)}, u32[]{:S(2)}, u32[]{:S(2)}) collective-permute-start(bf16[48,2304]{1,0:T(8,128)(2,1)} %get-tuple-element.88), channel_id=1, source_target_pairs={{0,1},{1,0},{2,3},{3,2},{4,5},{5,4},{6,7},{7,6},{8,9},{9,8},{10,11... | collective-permute-start | bytes 663560 | tf_op jit(solution)/shard_map/ppermute | solution.py:32
  127.3 14.3 %collective-permute-start.33 = (bf16[48,2304]{1,0:T(8,128)(2,1)S(1)}, bf16[48,2304]{1,0:T(8,128)(2,1)S(1)}, u32[]{:S(2)}, u32[]{:S(2)}) collective-permute-start(bf16[48,2304]{1,0:T(8,128)(2,1)S(1)} %fusion.2), channel_id=1, source_target_pairs={{0,6},{1,7},{2,4},{3,5},{4,2},{5,3},{6,0},{7,1},{8,14},{9,15},{10,... | collective-permute-start | bytes 663560 | tf_op jit(solution)/shard_map/ppermute | solution.py:32
  133.0 17.0 %collective-permute-start.34 = (bf16[48,2304]{1,0:T(8,128)(2,1)S(1)}, bf16[48,2304]{1,0:T(8,128)(2,1)S(1)}, u32[]{:S(2)}, u32[]{:S(2)}) collective-permute-start(bf16[48,2304]{1,0:T(8,128)(2,1)S(1)} %fusion.1), channel_id=1, source_target_pairs={{0,4},{1,5},{2,6},{3,7},{4,0},{5,1},{6,2},{7,3},{8,12},{9,13},{10,... | collective-permute-start | bytes 663560 | tf_op jit(solution)/shard_map/ppermute | solution.py:32
  138.9 11.3 %collective-permute-start.35 = (bf16[48,2304]{1,0:T(8,128)(2,1)S(1)}, bf16[48,2304]{1,0:T(8,128)(2,1)S(1)}, u32[]{:S(2)}, u32[]{:S(2)}) collective-permute-start(bf16[48,2304]{1,0:T(8,128)(2,1)S(1)} %fusion), channel_id=1, source_target_pairs={{0,2},{1,3},{2,0},{3,1},{4,6},{5,7},{6,4},{7,5},{8,10},{9,11},{10,... | collective-permute-start | bytes 663560 | tf_op jit(solution)/shard_map/ppermute | solution.py:32
  152.8 8.2 %collective-permute-start.39 = (bf16[48,2304]{1,0:T(8,128)(2,1)S(1)}, bf16[48,2304]{1,0:T(8,128)(2,1)S(1)}, u32[]{:S(2)}, u32[]{:S(2)}) collective-permute-start(bf16[48,2304]{1,0:T(8,128)(2,1)S(1)} %get-tuple-element.97.refs_1_.refs_0_), channel_id=1, source_target_pairs={{0,2},{1,3},{2,0},{3,1},{4,6},{5,7},{6,4},{7,5},{8,10},{9,11},{10,... | collective-permute-start | bytes 663560 | tf_op jit(solution)/shard_map/ppermute | solution.py:32
  152.8 11.8 %collective-permute-start.37 = (bf16[48,2304]{1,0:T(8,128)(2,1)S(1)}, bf16[48,2304]{1,0:T(8,128)(2,1)S(1)}, u32[]{:S(2)}, u32[]{:S(2)}) collective-permute-start(bf16[48,2304]{1,0:T(8,128)(2,1)S(1)} %get-tuple-element.97.refs_1_.refs_0_), channel_id=1, source_target_pairs={{0,6},{1,7},{2,4},{3,5},{4,2},{5,3},{6,0},{7,1},{8,14},{9,15},{10,... | collective-permute-start | bytes 663560 | tf_op jit(solution)/shard_map/ppermute | solution.py:32
  161.1 8.0 %collective-permute-start.40 = (bf16[48,2304]{1,0:T(8,128)(2,1)S(1)}, bf16[48,2304]{1,0:T(8,128)(2,1)S(1)}, u32[]{:S(2)}, u32[]{:S(2)}) collective-permute-start(bf16[48,2304]{1,0:T(8,128)(2,1)S(1)} %collective-permute-done.39.refs_1_.refs_4_), channel_id=1, source_target_pairs={{0,1},{1,0},{2,3},{3,2},{4,5},{5,4},{6,7},{7,6},{8,9},{9,8},{10,11... | collective-permute-start | bytes 663560 | tf_op jit(solution)/shard_map/ppermute | solution.py:32
  164.7 10.3 %collective-permute-start.41 = (bf16[48,2304]{1,0:T(8,128)(2,1)S(1)}, bf16[48,2304]{1,0:T(8,128)(2,1)S(1)}, u32[]{:S(2)}, u32[]{:S(2)}) collective-permute-start(bf16[48,2304]{1,0:T(8,128)(2,1)S(1)} %get-tuple-element.97.refs_1_.refs_0_), channel_id=1, source_target_pairs={{0,4},{1,5},{2,6},{3,7},{4,0},{5,1},{6,2},{7,3},{8,12},{9,13},{10,... | collective-permute-start | bytes 663560 | tf_op jit(solution)/shard_map/ppermute | solution.py:32
  183.1 8.7 %collective-permute-start.46 = (f32[96,1024]{1,0:T(8,128)S(1)}, f32[96,1024]{1,0:T(8,128)S(1)}, u32[]{:S(2)}, u32[]{:S(2)}) collective-permute-start(f32[96,1024]{1,0:T(8,128)S(1)} %shard_map.121.a0), channel_id=1, source_target_pairs={{0,8},{8,0},{1,9},{9,1},{2,10},{10,2},{3,11},{11,3},{4,12},{12,4},... | collective-permute-start | bytes 1179656 | tf_op jit(solution)/shard_map/ppermute | solution.py:36
  (30 other events, 212.4 us)

commit v4 on v3

--- a/solution.py
+++ b/solution.py
@@ -30,6 +30,10 @@
 
 def swap(x, k):
     return lax.ppermute(x, "lat", [(i, i ^ k) for i in range(8)])
+
+
+def send_z(x, pairs):
+    return lax.ppermute(x, "lat", [(2 * a + y, 2 * b + y) for a, b in pairs for y in range(2)])
 
 
 def pair(x, axis):
@@ -325,12 +329,13 @@
 def scatter(a, b):
     keep, send0, send3 = a
     got3 = swap(send3, 1)
-    s3 = swap(plus(keep[1], got3).astype(BF16), 6)
+    t3 = plus(keep[1], got3).astype(BF16)
+    inward, s3 = send_z(t3, ((0, 1), (3, 2))), send_z(t3, ((1, 2), (2, 1)))
     keep0, (keep, send1, send2) = keep[0], b
     got2 = swap(after(send2, got3), 1)
     got1 = swap(after(send1, got2), 1)
     s = plus(plus(keep0, swap(after(send0, got1), 1)), s3)
-    t2 = plus(keep[1], got2).astype(BF16)
+    t2 = plus(plus(keep[1], got2), inward).astype(BF16)
     s2 = swap(t2, 4)
     s1 = swap(plus(keep[0], after(got1, t2)).astype(BF16), 2)
     return plus(add(s, s2, MEDIUM), s1)

time: 195 us -> 191 us (0.979)
  waiting for transfers between devices: 71.7 us -> 63.7 us
  starting transfers between devices: 69.2 us -> 72.5 us
    ppermute x0 -> x4, starting transfers between devices: none -> 10.5 us  [send_z(): lax.ppermute(x, 'lat', [(2 * a + y, 2 * b + y) for a, b in pairs for y in...]
    ppermute x35 -> x33, waiting for transfers between devices: 61.1 us -> 50.8 us  [swap(): return lax.ppermute(x, 'lat', [(i, i ^ k) for i in range(8)])]
    ppermute x35 -> x33, starting transfers between devices: 61.4 us -> 53.9 us  [swap(): return lax.ppermute(x, 'lat', [(i, i ^ k) for i in range(8)])]
    ppermute x0 -> x4, waiting for transfers between devices: none -> 2.31 us  [send_z(): lax.ppermute(x, 'lat', [(2 * a + y, 2 * b + y) for a, b in pairs for y in...]
  transfers between devices with their start and end apart: 49 -> 51, of which waited for: 29 -> 26; matrix products, arithmetic and copies ran while one was open for 1% -> 1% of each run, Pallas kernels for 24% -> 24%
where the time goes in v4:
time: 191 us
  starting transfers between devices  72.5 us (38%)
  waiting for transfers between devices  63.7 us (33%)
  Pallas kernels  50.1 us (26%)
  other arithmetic  3.41 us (2%)
    ppermute x33, starting transfers between devices, swap(): return lax.ppermute(x, 'lat', [(i, i ^ k) for i in range(8)])  53.9 us
    ppermute x33, waiting for transfers between devices, swap(): return lax.ppermute(x, 'lat', [(i, i ^ k) for i in range(8)])  50.8 us
    pallas_call x15, Pallas kernels, vmem_call(): pl.pallas_call(lambda *refs: kernel(*refs[k:]), in_specs=[pl.BlockSpec(me...  26 us
    pallas_call x3, Pallas kernels, load(): pl.pallas_call(load_kernel, in_specs=[pl.BlockSpec(memory_space=pltpu.HBM...  12.1 us
    ppermute x14, waiting for transfers between devices, pair(): return lax.ppermute(x, axis, SWAP2)  10.7 us
    ppermute x4, starting transfers between devices, send_z(): lax.ppermute(x, 'lat', [(2 * a + y, 2 * b + y) for a, b in pairs for y in...  10.5 us
    ppermute x14, starting transfers between devices, pair(): return lax.ppermute(x, axis, SWAP2)  8.16 us
    pallas_call x1, Pallas kernels, decoder_grad(): call(grad_kernel, (n // step,), [cspec, cspec] + [whole(blocks[0])] * 8 +...  5.45 us
  transfers between devices with their start and end apart: 51, of which 26 were waited for; matrix products, arithmetic and copies ran while one was open for 1% of the time, Pallas kernels for 24%

profile of v4, /device:TPU:0, one launch (start us, length us, event | category | flops | bytes accessed | tf_op | source)
XLA Modules:
  0.0 191.0 jit_solution(17366525491227566021)
XLA Ops:
  0.6 3.1 %collective-permute-start = (bf16[48,2304]{1,0:T(8,128)(2,1)}, bf16[48,2304]{1,0:T(8,128)(2,1)S(1)}, u32[]{:S(2)}, u32[]{:S(2)}) collective-permute-start(bf16[48,2304]{1,0:T(8,128)(2,1)} %bitcast.52), channel_id=1, source_target_pairs={{0,2},{1,3},{2,0},{3,1},{4,6},{5,7},{6,4},{7,5},{8,10},{9,11},{10,... | collective-permute-start | bytes 663560 | tf_op jit(solution)/shard_map/ppermute | solution.py:32
  7.8 4.0 %shard_map.103.refs_4_ = bf16[2304,2304]{1,0:T(8,128)(2,1)S(1)} custom-call(bf16[2304,2304]{1,0:T(8,128)(2,1)} %bitcast.59), custom_call_target="tpu_custom_call" | custom-call | flops 1000 | bytes 1000 | tf_op jit(solution)/shard_map/pallas_call | solution.py:112
  11.9 4.0 %shard_map.104.refs_5_ = bf16[2304,2304]{1,0:T(8,128)(2,1)S(1)} custom-call(bf16[2304,2304]{1,0:T(8,128)(2,1)} %bitcast.60), custom_call_target="tpu_custom_call" | custom-call | flops 1000 | bytes 1000 | tf_op jit(solution)/shard_map/pallas_call | solution.py:112
  19.1 4.1 %shard_map.105.refs_2_ = bf16[2304,2304]{1,0:T(8,128)(2,1)S(1)} custom-call(bf16[2304,2304]{1,0:T(8,128)(2,1)} %bitcast.61), custom_call_target="tpu_custom_call" | custom-call | flops 1000 | bytes 1000 | tf_op jit(solution)/shard_map/pallas_call | solution.py:112
  23.1 4.0 %collective-permute-done.3.refs_2_ = bf16[48,2304]{1,0:T(8,128)(2,1)S(1)} collective-permute-done((bf16[48,2304]{1,0:T(8,128)(2,1)}, bf16[48,2304]{1,0:T(8,128)(2,1)S(1)}, u32[]{:S(2)}, u32[]{:S(2)}) %collective-permute-start.3) | collective-permute-done | bytes 221216 | tf_op jit(solution)/shard_map/ppermute | solution.py:32
  27.7 4.7 %shard_map.106.refs_0_ = bf16[2,192,2304]{2,1,0:T(8,128)(2,1)S(1)} custom-call(bf16[48,2304]{1,0:T(8,128)(2,1)S(1)} %bitcast.56, bf16[48,2304]{1,0:T(8,128)(2,1)S(1)} %collective-permute-done.1.refs_1_, bf16[48,2304]{1,0:T(8,128)(2,1)S(1)} %collective-permute-done.4.refs_2_, bf16[48,2304]{1,0:T(8,128)(2,1)S(1)} %collective-permute-done.5.refs_3_, ...), custom_call_target="tpu_custom_call" | custom-call | flops 1000 | bytes 1000 | tf_op jit(solution)/shard_map/pallas_call | solution.py:92
  33.1 4.7 %shard_map.107.refs_0_ = bf16[2,192,2304]{2,1,0:T(8,128)(2,1)S(1)} custom-call(bf16[48,2304]{1,0:T(8,128)(2,1)S(1)} %collective-permute-done.refs_0_, bf16[48,2304]{1,0:T(8,128)(2,1)S(1)} %collective-permute-done.2.refs_1_, bf16[48,2304]{1,0:T(8,128)(2,1)S(1)} %collective-permute-done.3.refs_2_, bf16[48,2304]{1,0:T(8,128)(2,1)S(1)} %collective-permute-done.7.refs_3_, ...), custom_call_target="tpu_custom_call" | custom-call | flops 1000 | bytes 1000 | tf_op jit(solution)/shard_map/pallas_call | solution.py:92
  38.0 3.6 %shard_map.108 = (f32[2,48,2304]{2,1,0:T(8,128)S(1)}, bf16[48,2304]{1,0:T(8,128)(2,1)S(1)}, bf16[48,2304]{1,0:T(8,128)(2,1)S(1)}) custom-call(bf16[2,192,2304]{2,1,0:T(8,128)(2,1)S(1)} %shard_map.106.refs_0_, bf16[2,192,2304]{2,1,0:T(8,128)(2,1)S(1)} %collective-permute-done.6.refs_1_, bf16[2304,2304]{1,0:T(8,128)(2,1)S(1)} %shard_map.105.refs_2_), custom_call_target="tpu_custom_call" | custom-call | flops 1000 | bytes 1000 | tf_op jit(solution)/shard_map/pallas_call | solution.py:92
  43.0 3.6 %shard_map.109 = (f32[2,48,2304]{2,1,0:T(8,128)S(1)}, bf16[48,2304]{1,0:T(8,128)(2,1)S(1)}, bf16[48,2304]{1,0:T(8,128)(2,1)S(1)}) custom-call(bf16[2,192,2304]{2,1,0:T(8,128)(2,1)S(1)} %shard_map.107.refs_0_, bf16[2,192,2304]{2,1,0:T(8,128)(2,1)S(1)} %collective-permute-done.8.refs_1_, bf16[2304,2304]{1,0:T(8,128)(2,1)S(1)} %shard_map.105.refs_2_), custom_call_target="tpu_custom_call" | custom-call | flops 1000 | bytes 1000 | tf_op jit(solution)/shard_map/pallas_call | solution.py:92
  50.4 5.5 %collective-permute-start.14 = (bf16[48,2304]{1,0:T(8,128)(2,1)S(1)}, bf16[48,2304]{1,0:T(8,128)(2,1)S(1)}, u32[]{:S(2)}, u32[]{:S(2)}) collective-permute-start(bf16[48,2304]{1,0:T(8,128)(2,1)S(1)} %fusion.8), channel_id=1, source_target_pairs={{0,2},{1,3},{6,4},{7,5},{8,10},{9,11},{14,12},{15,13},{16,18},{17,... | collective-permute-start | bytes 663560 | tf_op jit(solution)/shard_map/ppermute | solution.py:36
  60.0 3.4 %collective-permute-start.15 = (bf16[48,2304]{1,0:T(8,128)(2,1)S(1)}, bf16[48,2304]{1,0:T(8,128)(2,1)S(1)}, u32[]{:S(2)}, u32[]{:S(2)}) collective-permute-start(bf16[48,2304]{1,0:T(8,128)(2,1)S(1)} %fusion.7), channel_id=1, source_target_pairs={{0,4},{1,5},{2,6},{3,7},{4,0},{5,1},{6,2},{7,3},{8,12},{9,13},{10,... | collective-permute-start | bytes 663560 | tf_op jit(solution)/shard_map/ppermute | solution.py:32
  69.4 3.2 %collective-permute-done.15.refs_1_ = bf16[48,2304]{1,0:T(8,128)(2,1)S(1)} collective-permute-done((bf16[48,2304]{1,0:T(8,128)(2,1)S(1)}, bf16[48,2304]{1,0:T(8,128)(2,1)S(1)}, u32[]{:S(2)}, u32[]{:S(2)}) %collective-permute-start.15) | collective-permute-done | bytes 221216 | tf_op jit(solution)/shard_map/ppermute | solution.py:32
  77.5 4.7 %collective-permute-done.17.refs_1_ = bf16[48,2304]{1,0:T(8,128)(2,1)S(1)} collective-permute-done((bf16[48,2304]{1,0:T(8,128)(2,1)S(1)}, bf16[48,2304]{1,0:T(8,128)(2,1)S(1)}, u32[]{:S(2)}, u32[]{:S(2)}) %collective-permute-start.17) | collective-permute-done | bytes 221216 | tf_op jit(solution)/shard_map/ppermute | solution.py:32
  82.3 3.3 %collective-permute-start.19 = (bf16[48,2304]{1,0:T(8,128)(2,1)S(1)}, bf16[48,2304]{1,0:T(8,128)(2,1)S(1)}, u32[]{:S(2)}, u32[]{:S(2)}) collective-permute-start(bf16[48,2304]{1,0:T(8,128)(2,1)S(1)} %collective-permute-done.17.refs_1_), channel_id=1, source_target_pairs={{0,1},{1,0},{2,3},{3,2},{4,5},{5,4},{6,7},{7,6},{8,9},{9,8},{10,11... | collective-permute-start | bytes 663560 | tf_op jit(solution)/shard_map/ppermute | solution.py:32
  85.7 4.9 %collective-permute-start.25 = (bf16[48,2304]{1,0:T(8,128)(2,1)S(1)}, bf16[48,2304]{1,0:T(8,128)(2,1)S(1)}, u32[]{:S(2)}, u32[]{:S(2)}) collective-permute-start(bf16[48,2304]{1,0:T(8,128)(2,1)S(1)} %add_convert_fusion.refs_1_), channel_id=1, source_target_pairs={{0,4},{1,5},{2,6},{3,7},{4,0},{5,1},{6,2},{7,3},{8,12},{9,13},{10,... | collective-permute-start | bytes 663560 | tf_op jit(solution)/shard_map/ppermute | solution.py:32
  107.3 5.5 %collective-permute-done.28.refs_1_ = bf16[96,1024]{1,0:T(8,128)(2,1)S(1)} collective-permute-done((bf16[96,1024]{1,0:T(8,128)(2,1)S(1)}, bf16[96,1024]{1,0:T(8,128)(2,1)S(1)}, u32[]{:S(2)}, u32[]{:S(2)}) %collective-permute-start.28) | collective-permute-done | bytes 196640 | tf_op jit(solution)/shard_map/ppermute | solution.py:40
  118.5 5.8 %collective-permute-done.30 = bf16[48,2304]{1,0:T(8,128)(2,1)S(1)} collective-permute-done((bf16[48,2304]{1,0:T(8,128)(2,1)S(1)}, bf16[48,2304]{1,0:T(8,128)(2,1)S(1)}, u32[]{:S(2)}, u32[]{:S(2)}) %collective-permute-start.30) | collective-permute-done | bytes 221216 | tf_op jit(solution)/shard_map/ppermute | solution.py:32
  126.7 3.5 %collective-permute-start.35 = (bf16[48,2304]{1,0:T(8,128)(2,1)}, bf16[48,2304]{1,0:T(8,128)(2,1)}, u32[]{:S(2)}, u32[]{:S(2)}) collective-permute-start(bf16[48,2304]{1,0:T(8,128)(2,1)} %fusion.3), channel_id=1, source_target_pairs={{0,2},{1,3},{6,4},{7,5},{8,10},{9,11},{14,12},{15,13},{16,18},{17,... | collective-permute-start | bytes 663560 | tf_op jit(solution)/shard_map/ppermute | solution.py:36
  134.8 3.0 %collective-permute-start.36 = (bf16[48,2304]{1,0:T(8,128)(2,1)S(1)}, bf16[48,2304]{1,0:T(8,128)(2,1)S(1)}, u32[]{:S(2)}, u32[]{:S(2)}) collective-permute-start(bf16[48,2304]{1,0:T(8,128)(2,1)S(1)} %fusion.2), channel_id=1, source_target_pairs={{0,4},{1,5},{2,6},{3,7},{4,0},{5,1},{6,2},{7,3},{8,12},{9,13},{10,... | collective-permute-start | bytes 663560 | tf_op jit(solution)/shard_map/ppermute | solution.py:32
  140.0 3.8 %collective-permute-done.33 = bf16[48,2304]{1,0:T(8,128)(2,1)S(1)} collective-permute-done((bf16[48,2304]{1,0:T(8,128)(2,1)S(1)}, bf16[48,2304]{1,0:T(8,128)(2,1)S(1)}, u32[]{:S(2)}, u32[]{:S(2)}) %collective-permute-start.33) | collective-permute-done | bytes 221216 | tf_op jit(solution)/shard_map/ppermute | solution.py:32
  152.5 3.0 %collective-permute-done.38.refs_2_.refs_1_ = bf16[48,2304]{1,0:T(8,128)(2,1)S(1)} collective-permute-done((bf16[48,2304]{1,0:T(8,128)(2,1)S(1)}, bf16[48,2304]{1,0:T(8,128)(2,1)S(1)}, u32[]{:S(2)}, u32[]{:S(2)}) %collective-permute-start.38) | collective-permute-done | bytes 221216 | tf_op jit(solution)/shard_map/ppermute | solution.py:32
  157.6 3.1 %collective-permute-done.39._.refs_3_.refs_2_ = bf16[48,2304]{1,0:T(8,128)(2,1)S(1)} collective-permute-done((bf16[48,2304]{1,0:T(8,128)(2,1)S(1)}, bf16[48,2304]{1,0:T(8,128)(2,1)S(1)}, u32[]{:S(2)}, u32[]{:S(2)}) %collective-permute-start.39) | collective-permute-done | bytes 221216 | tf_op jit(solution)/shard_map/ppermute | solution.py:32
  160.6 3.5 %collective-permute-start.43 = (bf16[48,2304]{1,0:T(8,128)(2,1)S(1)}, bf16[48,2304]{1,0:T(8,128)(2,1)S(1)}, u32[]{:S(2)}, u32[]{:S(2)}) collective-permute-start(bf16[48,2304]{1,0:T(8,128)(2,1)S(1)} %get-tuple-element.97.refs_1_.refs_0_), channel_id=1, source_target_pairs={{0,4},{1,5},{2,6},{3,7},{4,0},{5,1},{6,2},{7,3},{8,12},{9,13},{10,... | collective-permute-start | bytes 663560 | tf_op jit(solution)/shard_map/ppermute | solution.py:32
  181.8 5.4 %shard_map.122 = (f32[18432,128]{1,0:T(8,128)}, f32[8,128]{1,0:T(8,128)S(1)}) custom-call(bf16[192,1024]{1,0:T(8,128)(2,1)S(1)} %get-tuple-element.94.c0, bf16[192,1024]{1,0:T(8,128)(2,1)S(1)} %get-tuple-element.95.c1, bf16[48,2304]{1,0:T(8,128)(2,1)S(1)} %get-tuple-element.97.refs_1_.refs_0_, bf16[48,2304]{1,0:T(8,128)(2,1)S(1)} %collective-permute-done.38.refs_2_.refs_1_, ...), custom_call_target="tpu_custom_call" | custom-call | flops 20000000000 | bytes 1000 | tf_op jit(solution)/shard_map/pallas_call | solution.py:286
  (127 shorter events, 92.2 us)
Async XLA Ops:
  0.6 15.3 %collective-permute-start = (bf16[48,2304]{1,0:T(8,128)(2,1)}, bf16[48,2304]{1,0:T(8,128)(2,1)S(1)}, u32[]{:S(2)}, u32[]{:S(2)}) collective-permute-start(bf16[48,2304]{1,0:T(8,128)(2,1)} %bitcast.52), channel_id=1, source_target_pairs={{0,2},{1,3},{2,0},{3,1},{4,6},{5,7},{6,4},{7,5},{8,10},{9,11},{10,... | collective-permute-start | bytes 663560 | tf_op jit(solution)/shard_map/ppermute | solution.py:32
  3.7 12.2 %collective-permute-start.1 = (bf16[48,2304]{1,0:T(8,128)(2,1)}, bf16[48,2304]{1,0:T(8,128)(2,1)S(1)}, u32[]{:S(2)}, u32[]{:S(2)}) collective-permute-start(bf16[48,2304]{1,0:T(8,128)(2,1)} %bitcast.53), channel_id=1, source_target_pairs={{0,1},{1,0},{2,3},{3,2},{4,5},{5,4},{6,7},{7,6},{8,9},{9,8},{10,11... | collective-permute-start | bytes 663560 | tf_op jit(solution)/shard_map/ppermute | solution.py:32
  5.2 12.3 %collective-permute-start.4 = (bf16[48,2304]{1,0:T(8,128)(2,1)}, bf16[48,2304]{1,0:T(8,128)(2,1)S(1)}, u32[]{:S(2)}, u32[]{:S(2)}) collective-permute-start(bf16[48,2304]{1,0:T(8,128)(2,1)} %bitcast.54), channel_id=1, source_target_pairs={{0,6},{1,7},{2,4},{3,5},{4,2},{5,3},{6,0},{7,1},{8,14},{9,15},{10,... | collective-permute-start | bytes 663560 | tf_op jit(solution)/shard_map/ppermute | solution.py:32
  7.7 19.4 %collective-permute-start.3 = (bf16[48,2304]{1,0:T(8,128)(2,1)}, bf16[48,2304]{1,0:T(8,128)(2,1)S(1)}, u32[]{:S(2)}, u32[]{:S(2)}) collective-permute-start(bf16[48,2304]{1,0:T(8,128)(2,1)} %bitcast.55), channel_id=1, source_target_pairs={{0,4},{1,5},{2,6},{3,7},{4,0},{5,1},{6,2},{7,3},{8,12},{9,13},{10,... | collective-permute-start | bytes 663560 | tf_op jit(solution)/shard_map/ppermute | solution.py:32
  15.9 11.7 %collective-permute-start.2 = (bf16[48,2304]{1,0:T(8,128)(2,1)S(1)}, bf16[48,2304]{1,0:T(8,128)(2,1)S(1)}, u32[]{:S(2)}, u32[]{:S(2)}) collective-permute-start(bf16[48,2304]{1,0:T(8,128)(2,1)S(1)} %collective-permute-done.refs_0_), channel_id=1, source_target_pairs={{0,1},{1,0},{2,3},{3,2},{4,5},{5,4},{6,7},{7,6},{8,9},{9,8},{10,11... | collective-permute-start | bytes 663560 | tf_op jit(solution)/shard_map/ppermute | solution.py:32
  17.5 10.1 %collective-permute-start.5 = (bf16[48,2304]{1,0:T(8,128)(2,1)S(1)}, bf16[48,2304]{1,0:T(8,128)(2,1)S(1)}, u32[]{:S(2)}, u32[]{:S(2)}) collective-permute-start(bf16[48,2304]{1,0:T(8,128)(2,1)S(1)} %collective-permute-done.4.refs_2_), channel_id=1, source_target_pairs={{0,1},{1,0},{2,3},{3,2},{4,5},{5,4},{6,7},{7,6},{8,9},{9,8},{10,11... | collective-permute-start | bytes 663560 | tf_op jit(solution)/shard_map/ppermute | solution.py:32
  41.6 7.9 %collective-permute-start.9 = (bf16[48,2304]{1,0:T(8,128)(2,1)S(1)}, bf16[48,2304]{1,0:T(8,128)(2,1)S(1)}, u32[]{:S(2)}, u32[]{:S(2)}) collective-permute-start(bf16[48,2304]{1,0:T(8,128)(2,1)S(1)} %get-tuple-element.69), channel_id=1, source_target_pairs={{0,1},{1,0},{2,3},{3,2},{4,5},{5,4},{6,7},{7,6},{8,9},{9,8},{10,11... | collective-permute-start | bytes 663560 | tf_op jit(solution)/shard_map/ppermute | solution.py:32
  50.4 9.5 %collective-permute-start.14 = (bf16[48,2304]{1,0:T(8,128)(2,1)S(1)}, bf16[48,2304]{1,0:T(8,128)(2,1)S(1)}, u32[]{:S(2)}, u32[]{:S(2)}) collective-permute-start(bf16[48,2304]{1,0:T(8,128)(2,1)S(1)} %fusion.8), channel_id=1, source_target_pairs={{0,2},{1,3},{6,4},{7,5},{8,10},{9,11},{14,12},{15,13},{16,18},{17,... | collective-permute-start | bytes 663560 | tf_op jit(solution)/shard_map/ppermute | solution.py:36
  55.9 10.9 %collective-permute-start.13 = (bf16[48,2304]{1,0:T(8,128)(2,1)S(1)}, bf16[48,2304]{1,0:T(8,128)(2,1)S(1)}, u32[]{:S(2)}, u32[]{:S(2)}) collective-permute-start(bf16[48,2304]{1,0:T(8,128)(2,1)S(1)} %fusion.8), channel_id=1, source_target_pairs={{2,4},{3,5},{4,2},{5,3},{10,12},{11,13},{12,10},{13,11},{18,20},{1... | collective-permute-start | bytes 663560 | tf_op jit(solution)/shard_map/ppermute | solution.py:36
  60.0 12.7 %collective-permute-start.15 = (bf16[48,2304]{1,0:T(8,128)(2,1)S(1)}, bf16[48,2304]{1,0:T(8,128)(2,1)S(1)}, u32[]{:S(2)}, u32[]{:S(2)}) collective-permute-start(bf16[48,2304]{1,0:T(8,128)(2,1)S(1)} %fusion.7), channel_id=1, source_target_pairs={{0,4},{1,5},{2,6},{3,7},{4,0},{5,1},{6,2},{7,3},{8,12},{9,13},{10,... | collective-permute-start | bytes 663560 | tf_op jit(solution)/shard_map/ppermute | solution.py:32
  64.9 9.1 %collective-permute-start.16 = (bf16[48,2304]{1,0:T(8,128)(2,1)S(1)}, bf16[48,2304]{1,0:T(8,128)(2,1)S(1)}, u32[]{:S(2)}, u32[]{:S(2)}) collective-permute-start(bf16[48,2304]{1,0:T(8,128)(2,1)S(1)} %fusion.5), channel_id=1, source_target_pairs={{0,2},{1,3},{2,0},{3,1},{4,6},{5,7},{6,4},{7,5},{8,10},{9,11},{10,... | collective-permute-start | bytes 663560 | tf_op jit(solution)/shard_map/ppermute | solution.py:32
  74.0 8.2 %collective-permute-start.17 = (bf16[48,2304]{1,0:T(8,128)(2,1)S(1)}, bf16[48,2304]{1,0:T(8,128)(2,1)S(1)}, u32[]{:S(2)}, u32[]{:S(2)}) collective-permute-start(bf16[48,2304]{1,0:T(8,128)(2,1)S(1)} %add_convert_fusion.refs_1_), channel_id=1, source_target_pairs={{0,2},{1,3},{2,0},{3,1},{4,6},{5,7},{6,4},{7,5},{8,10},{9,11},{10,... | collective-permute-start | bytes 663560 | tf_op jit(solution)/shard_map/ppermute | solution.py:32
  74.1 8.2 %collective-permute-start.18 = (bf16[48,2304]{1,0:T(8,128)(2,1)S(1)}, bf16[48,2304]{1,0:T(8,128)(2,1)S(1)}, u32[]{:S(2)}, u32[]{:S(2)}) collective-permute-start(bf16[48,2304]{1,0:T(8,128)(2,1)S(1)} %add_convert_fusion.refs_1_), channel_id=1, source_target_pairs={{0,1},{1,0},{2,3},{3,2},{4,5},{5,4},{6,7},{7,6},{8,9},{9,8},{10,11... | collective-permute-start | bytes 663560 | tf_op jit(solution)/shard_map/ppermute | solution.py:32
  75.3 10.3 %collective-permute-start.20 = (bf16[48,2304]{1,0:T(8,128)(2,1)S(1)}, bf16[48,2304]{1,0:T(8,128)(2,1)S(1)}, u32[]{:S(2)}, u32[]{:S(2)}) collective-permute-start(bf16[48,2304]{1,0:T(8,128)(2,1)S(1)} %add_convert_fusion.refs_1_), channel_id=1, source_target_pairs={{0,6},{1,7},{2,4},{3,5},{4,2},{5,3},{6,0},{7,1},{8,14},{9,15},{10,... | collective-permute-start | bytes 663560 | tf_op jit(solution)/shard_map/ppermute | solution.py:32
  82.3 10.8 %collective-permute-start.19 = (bf16[48,2304]{1,0:T(8,128)(2,1)S(1)}, bf16[48,2304]{1,0:T(8,128)(2,1)S(1)}, u32[]{:S(2)}, u32[]{:S(2)}) collective-permute-start(bf16[48,2304]{1,0:T(8,128)(2,1)S(1)} %collective-permute-done.17.refs_1_), channel_id=1, source_target_pairs={{0,1},{1,0},{2,3},{3,2},{4,5},{5,4},{6,7},{7,6},{8,9},{9,8},{10,11... | collective-permute-start | bytes 663560 | tf_op jit(solution)/shard_map/ppermute | solution.py:32
  85.7 11.2 %collective-permute-start.25 = (bf16[48,2304]{1,0:T(8,128)(2,1)S(1)}, bf16[48,2304]{1,0:T(8,128)(2,1)S(1)}, u32[]{:S(2)}, u32[]{:S(2)}) collective-permute-start(bf16[48,2304]{1,0:T(8,128)(2,1)S(1)} %add_convert_fusion.refs_1_), channel_id=1, source_target_pairs={{0,4},{1,5},{2,6},{3,7},{4,0},{5,1},{6,2},{7,3},{8,12},{9,13},{10,... | collective-permute-start | bytes 663560 | tf_op jit(solution)/shard_map/ppermute | solution.py:32
  130.2 9.8 %collective-permute-start.34 = (bf16[48,2304]{1,0:T(8,128)(2,1)}, bf16[48,2304]{1,0:T(8,128)(2,1)S(1)}, u32[]{:S(2)}, u32[]{:S(2)}) collective-permute-start(bf16[48,2304]{1,0:T(8,128)(2,1)} %fusion.3), channel_id=1, source_target_pairs={{2,4},{3,5},{4,2},{5,3},{10,12},{11,13},{12,10},{13,11},{18,20},{1... | collective-permute-start | bytes 663560 | tf_op jit(solution)/shard_map/ppermute | solution.py:36
  134.8 11.6 %collective-permute-start.36 = (bf16[48,2304]{1,0:T(8,128)(2,1)S(1)}, bf16[48,2304]{1,0:T(8,128)(2,1)S(1)}, u32[]{:S(2)}, u32[]{:S(2)}) collective-permute-start(bf16[48,2304]{1,0:T(8,128)(2,1)S(1)} %fusion.2), channel_id=1, source_target_pairs={{0,4},{1,5},{2,6},{3,7},{4,0},{5,1},{6,2},{7,3},{8,12},{9,13},{10,... | collective-permute-start | bytes 663560 | tf_op jit(solution)/shard_map/ppermute | solution.py:32
  139.5 8.0 %collective-permute-start.37 = (bf16[48,2304]{1,0:T(8,128)(2,1)S(1)}, bf16[48,2304]{1,0:T(8,128)(2,1)S(1)}, u32[]{:S(2)}, u32[]{:S(2)}) collective-permute-start(bf16[48,2304]{1,0:T(8,128)(2,1)S(1)} %fusion), channel_id=1, source_target_pairs={{0,2},{1,3},{2,0},{3,1},{4,6},{5,7},{6,4},{7,5},{8,10},{9,11},{10,... | collective-permute-start | bytes 663560 | tf_op jit(solution)/shard_map/ppermute | solution.py:32
  149.1 8.0 %collective-permute-start.41 = (bf16[48,2304]{1,0:T(8,128)(2,1)S(1)}, bf16[48,2304]{1,0:T(8,128)(2,1)S(1)}, u32[]{:S(2)}, u32[]{:S(2)}) collective-permute-start(bf16[48,2304]{1,0:T(8,128)(2,1)S(1)} %get-tuple-element.97.refs_1_.refs_0_), channel_id=1, source_target_pairs={{0,2},{1,3},{2,0},{3,1},{4,6},{5,7},{6,4},{7,5},{8,10},{9,11},{10,... | collective-permute-start | bytes 663560 | tf_op jit(solution)/shard_map/ppermute | solution.py:32
  150.5 10.1 %collective-permute-start.39 = (bf16[48,2304]{1,0:T(8,128)(2,1)S(1)}, bf16[48,2304]{1,0:T(8,128)(2,1)S(1)}, u32[]{:S(2)}, u32[]{:S(2)}) collective-permute-start(bf16[48,2304]{1,0:T(8,128)(2,1)S(1)} %get-tuple-element.97.refs_1_.refs_0_), channel_id=1, source_target_pairs={{0,6},{1,7},{2,4},{3,5},{4,2},{5,3},{6,0},{7,1},{8,14},{9,15},{10,... | collective-permute-start | bytes 663560 | tf_op jit(solution)/shard_map/ppermute | solution.py:32
  157.2 9.4 %collective-permute-start.42 = (bf16[48,2304]{1,0:T(8,128)(2,1)S(1)}, bf16[48,2304]{1,0:T(8,128)(2,1)S(1)}, u32[]{:S(2)}, u32[]{:S(2)}) collective-permute-start(bf16[48,2304]{1,0:T(8,128)(2,1)S(1)} %collective-permute-done.41.refs_1_.refs_4_), channel_id=1, source_target_pairs={{0,1},{1,0},{2,3},{3,2},{4,5},{5,4},{6,7},{7,6},{8,9},{9,8},{10,11... | collective-permute-start | bytes 663560 | tf_op jit(solution)/shard_map/ppermute | solution.py:32
  160.6 9.8 %collective-permute-start.43 = (bf16[48,2304]{1,0:T(8,128)(2,1)S(1)}, bf16[48,2304]{1,0:T(8,128)(2,1)S(1)}, u32[]{:S(2)}, u32[]{:S(2)}) collective-permute-start(bf16[48,2304]{1,0:T(8,128)(2,1)S(1)} %get-tuple-element.97.refs_1_.refs_0_), channel_id=1, source_target_pairs={{0,4},{1,5},{2,6},{3,7},{4,0},{5,1},{6,2},{7,3},{8,12},{9,13},{10,... | collective-permute-start | bytes 663560 | tf_op jit(solution)/shard_map/ppermute | solution.py:32
  178.4 9.0 %collective-permute-start.48 = (f32[96,1024]{1,0:T(8,128)S(1)}, f32[96,1024]{1,0:T(8,128)S(1)}, u32[]{:S(2)}, u32[]{:S(2)}) collective-permute-start(f32[96,1024]{1,0:T(8,128)S(1)} %shard_map.121.a0), channel_id=1, source_target_pairs={{0,8},{8,0},{1,9},{9,1},{2,10},{10,2},{3,11},{11,3},{4,12},{12,4},... | collective-permute-start | bytes 1179656 | tf_op jit(solution)/shard_map/ppermute | solution.py:40
  (32 other events, 239.7 us)
